TPU v7x, 256 devices: a whole 4x4x8 slice. The times are simulated.
256 devices in a mesh: dp: 4 (over x_hi, core), fsdp: 64 (over y, z, x_lo).
Axes of the slice: x: 4 (x_hi: 2, x_lo: 2; x = x_hi * 2 + x_lo), y: 4, z: 8, core: 2. Of those that a mesh axis runs over, the one named last changes fastest.
Arguments:
- gen_input: bfloat16 [32768, 2560], P(('dp', 'fsdp')), may hold values from -10 to 10
- noise: bfloat16 [32768, 2560], P(('dp', 'fsdp')), may hold values from -6 to 6
- dmd_step: int32 [2], replicated, may hold values from 20 to 980
- scale_group: int32 [3, 2], replicated, may hold values from 0 to 7
- gen_codes: bfloat16 [2560, 2560], P('fsdp', 'dp'), may hold values from -0.125 to 0.125
- teacher_codes: bfloat16 [2560, 2560], P('fsdp', 'dp'), may hold values from -0.125 to 0.125
- critic_codes: bfloat16 [2560, 2560], P('fsdp', 'dp'), may hold values from -0.125 to 0.125
- code_scales: float32 [3, 8, 2560], P(None, None, 'dp'), may hold values from 0.5 to 2
- modulation: float32 [3, 3, 2560], replicated, may hold values from -3 to 3
- time_proj: bfloat16 [2, 256, 7680], replicated, may hold values from -0.375 to 0.375
Outputs:
- sample: bfloat16 [32768, 2560], P(('dp', 'fsdp'))
- dmd_grad: bfloat16 [32768, 2560], P(('dp', 'fsdp'))
- weight_grad: float32 [2560, 2560], P('fsdp', 'dp')
All inputs are finite; a program needn't handle non-finite values.
Results may differ from a plain program's by a relative error of at most 0.012.
Values may be sent and summed in bfloat16 or wider, within the bound.
A program may use at most 128 MiB of HBM per device.

v0:
```python
import math

import jax
import jax.numpy as jnp
from jax import lax
from jax.sharding import PartitionSpec as P

RMS_EPS = 1e-06
SPREAD_EPS = 1e-05


def normalize(values):
    return values * lax.rsqrt(jnp.mean(values * values, axis=-1, keepdims=True) + RMS_EPS)


def time_features(timesteps, freq_count):
    freq_index = jnp.arange(freq_count, dtype=jnp.float32)
    frequency = jnp.exp(freq_index * (-math.log(10000.0) / freq_count))
    phase_angle = timesteps.astype(jnp.float32)[:, None] * frequency[None, :]
    return jnp.concatenate([jnp.cos(phase_angle), jnp.sin(phase_angle)], axis=1)


def judge_modulations(dmd_step, modulation, time_proj):
    features = time_features(dmd_step, time_proj.shape[1] // 2)
    lifted = jnp.einsum(
        "cf,mfe->mce", features, time_proj.astype(jnp.float32), precision=lax.Precision.HIGHEST
    )
    return modulation[1:, None] + lifted.reshape(2, dmd_step.shape[0], 3, modulation.shape[2])


def block_factor(product, factor, dp_size):
    column_count = product.shape[1]
    repeated = jnp.repeat(factor, dp_size // factor.shape[0], axis=0)
    scaled = product.reshape(dp_size, -1, column_count) * repeated[:, None, :]
    return scaled.reshape(-1, column_count)


def gather_group(stacked):
    return lax.all_gather(stacked, "dp", axis=1, tiled=True)


def return_tokens(stacked):
    return lax.all_to_all(stacked, "dp", split_axis=1, concat_axis=2, tiled=True)


def on_device(
    gen_input,
    noise,
    dmd_step,
    scale_group,
    gen_codes,
    teacher_codes,
    critic_codes,
    code_scales,
    modulation,
    time_proj,
):
    dp_size = lax.axis_size("dp")
    fsdp_size = lax.axis_size("fsdp")
    clip_count = dmd_step.shape[0]
    dp_per_clip = dp_size // clip_count
    tok_rows, model_width = gen_input.shape
    col_width = gen_codes.shape[1]
    group_count = code_scales.shape[1]
    dp_index = lax.axis_index("dp")
    own_clip = dp_index // dp_per_clip
    col_offset = dp_index * col_width
    clip_tokens = tok_rows * dp_size * fsdp_size // clip_count
    judge_mod = judge_modulations(dmd_step, modulation, time_proj)
    gen_mod = modulation[0]
    noise_levels = dmd_step.astype(jnp.float32) / 1000.0
    group_hot = (
        scale_group[:, :, None] == jnp.arange(group_count, dtype=jnp.int32)[None, None, :]
    ).astype(jnp.float32)
    scale_pick = jnp.einsum("mcg,mgd->mcd", group_hot, code_scales, precision=lax.Precision.HIGHEST)
    gen_gate = lax.dynamic_slice_in_dim(gen_mod[2], col_offset, col_width)
    gen_factor = gen_gate[None, :] * scale_pick[0]
    judge_gate = lax.dynamic_slice_in_dim(judge_mod[:, :, 2], col_offset, col_width, 2)
    judge_factor = judge_gate * scale_pick[1:]
    gen_full, teacher_full, critic_full = (
        lax.all_gather(gen_codes, "fsdp", axis=0, tiled=True),
        lax.all_gather(teacher_codes, "fsdp", axis=0, tiled=True),
        lax.all_gather(critic_codes, "fsdp", axis=0, tiled=True),
    )
    latent = gen_input.astype(jnp.float32)
    gen_hat = (normalize(latent) * (1.0 + gen_mod[1]) + gen_mod[0]).astype(jnp.bfloat16)
    hat_group = gather_group(gen_hat[None])[0]
    gen_product = jnp.dot(hat_group, gen_full, preferred_element_type=jnp.float32)
    gen_part = block_factor(gen_product, gen_factor, dp_size).astype(jnp.bfloat16)
    gen_branch = return_tokens(gen_part[None])[0]
    clean_est = latent + gen_branch.astype(jnp.float32)
    own_level = noise_levels[own_clip]
    noisy_latent = (1.0 - own_level) * clean_est + own_level * noise.astype(jnp.float32)
    normed = normalize(noisy_latent).astype(jnp.bfloat16)
    own_mod = jnp.take(judge_mod, own_clip, axis=1)
    local_hats = jnp.stack(
        [
            (
                normed.astype(jnp.float32) * (1.0 + own_mod[judge_index, 1])
                + own_mod[judge_index, 0]
            ).astype(jnp.bfloat16)
            for judge_index in range(2)
        ]
    )
    judge_hats = gather_group(local_hats)
    real_product = jnp.dot(judge_hats[0], teacher_full, preferred_element_type=jnp.float32)
    fake_product = jnp.dot(judge_hats[1], critic_full, preferred_element_type=jnp.float32)
    real_part = block_factor(real_product, judge_factor[0], dp_size).astype(jnp.bfloat16)
    fake_part = block_factor(fake_product, judge_factor[1], dp_size).astype(jnp.bfloat16)
    judged = return_tokens(jnp.stack([real_part, fake_part]))
    real_branch = judged[0].astype(jnp.float32)
    fake_branch = judged[1].astype(jnp.float32)
    real_clean = noisy_latent - own_level * (noisy_latent + real_branch)
    partial_value = jnp.sum(jnp.abs(clean_est - real_clean))
    clip_pick = (jnp.arange(clip_count, dtype=jnp.int32) == own_clip).astype(jnp.float32)
    totals = lax.psum(clip_pick * partial_value, ("dp", "fsdp"))
    spread = totals / (clip_tokens * model_width) + SPREAD_EPS
    score_gap = own_level * (real_branch - fake_branch) / spread[own_clip]
    block_level = jnp.repeat(noise_levels, dp_per_clip)[:, None, None]
    block_spread = jnp.repeat(spread, dp_per_clip)[:, None, None]
    branch_gap = (real_part.astype(jnp.float32) - fake_part.astype(jnp.float32)).reshape(
        dp_size, tok_rows, col_width
    )
    group_gap = (block_level * branch_gap / block_spread).reshape(dp_size * tok_rows, col_width)
    cotangent = block_factor(group_gap, gen_factor, dp_size).astype(jnp.bfloat16)
    grad_total = lax.psum_scatter(
        lax.dot_general(
            hat_group, cotangent, (((0,), (0,)), ((), ())), preferred_element_type=jnp.float32
        ),
        "fsdp",
        scatter_dimension=0,
        tiled=True,
    )
    weight_grad = grad_total / (tok_rows * dp_size * fsdp_size)
    return (clean_est.astype(jnp.bfloat16), score_gap.astype(jnp.bfloat16), weight_grad)


def solution(mesh):
    return jax.shard_map(
        on_device,
        mesh=mesh,
        in_specs=(
            P(("dp", "fsdp"), None),
            P(("dp", "fsdp"), None),
            P(),
            P(),
            P("fsdp", "dp"),
            P("fsdp", "dp"),
            P("fsdp", "dp"),
            P(None, None, "dp"),
            P(),
            P(),
        ),
        out_specs=(P(("dp", "fsdp"), None), P(("dp", "fsdp"), None), P("fsdp", "dp")),
        check_vma=False,
    )
```

profile of v0, /device:TPU:8, one launch (start us, length us, event | category | flops | bytes accessed | tf_op | source)
XLA Modules:
  0.0 1465.3 jit_solution(13775428794132267867)
XLA Ops:
  10.0 2.2 fusion.31
  13.5 6.4 convolution_bitcast_fusion
  20.1 27.6 %all-gather.15.cloned.1.call-done = bf16[512,2560]{0,1:T(8,128)(2,1)} async-done(((bf16[128,2560]{0,1:T(8,128)(2,1)}), bf16[512,2560]{0,1:T(8,128)(2,1)}) %all-gather.15.cloned.1.call-update) | async-done | bytes 2621456 | tf_op jit(solution)/shard_map/all_gather | solution.py:39
  47.7 3.0 copy.35
  50.7 278.2 %all-gather.7.cloned.1.call-done = bf16[2560,640]{1,0:T(8,128)(2,1)} async-done(((bf16[40,640]{1,0:T(8,128)(2,1)}), bf16[2560,640]{1,0:T(8,128)(2,1)}) %all-gather.7.cloned.1.call-update) | async-done | bytes 3276816 | tf_op jit(solution)/shard_map/all_gather | solution.py:81
  328.9 4.1 fusion.21
  334.6 4.8 reduce.14
  340.4 4.4 all-to-all-start
  346.5 10.0 all-to-all-done
  358.4 2.6 copy.38
  368.2 63.9 %all-gather.9.cloned.1.call-done = bf16[2,512,2560]{1,2,0:T(8,128)(2,1)} async-done(((bf16[2,128,2560]{1,2,0:T(8,128)(2,1)}), bf16[2,512,2560]{1,2,0:T(8,128)(2,1)}) %all-gather.9.cloned.1.call-update) | async-done | bytes 5242896 | tf_op jit(solution)/shard_map/all_gather | solution.py:39
  432.1 5.2 fusion.53
  437.3 4.4 copy.40
  441.7 271.5 %all-gather.11.cloned.1.call-done = bf16[2560,640]{1,0:T(8,128)(2,1)} async-done(((bf16[40,640]{1,0:T(8,128)(2,1)}), bf16[2560,640]{1,0:T(8,128)(2,1)}) %all-gather.11.cloned.1.call-update) | async-done | bytes 3276816 | tf_op jit(solution)/shard_map/all_gather | solution.py:82
  713.2 4.9 fusion.18
  720.0 4.4 copy.41
  724.4 290.4 %all-gather.13.cloned.1.call-done = bf16[2560,640]{1,0:T(8,128)(2,1)} async-done(((bf16[40,640]{1,0:T(8,128)(2,1)}), bf16[2560,640]{1,0:T(8,128)(2,1)}) %all-gather.13.cloned.1.call-update) | async-done | bytes 3276816 | tf_op jit(solution)/shard_map/all_gather | solution.py:83
  1014.8 4.9 fusion.15
  1021.6 3.0 pad_maximum_fusion.1
  1024.5 23.0 %all_to_all.24 = bf16[2,512,640]{2,0,1:T(2,128)(2,1)S(1)} all-to-all(bf16[2,512,640]{2,0,1:T(2,128)(2,1)S(1)} %pad_maximum_fusion.1), channel_id=1, replica_groups=mesh['dp'=4,'fsdp'=64] {'dp'}, dimensions={1} | all-to-all | bytes 2621440 | tf_op jit(solution)/shard_map/all_to_all | solution.py:43
  1051.1 3.9 fusion.39
  1055.8 96.6 %psum.7 = f32[2]{0:T(128)S(1)} all-reduce(f32[2]{0:T(128)S(1)} %compare_select_fusion), channel_id=1, replica_groups=mesh['dp'=4,'fsdp'=64] {'dp','fsdp'}, use_global_device_ids=true, to_apply=%region_3.4 | all-reduce | flops 2 | bytes 16 | tf_op jit(solution)/shard_map/psum | solution.py:116
  1154.1 6.7 fusion.54
  1166.9 290.0 %reduce-scatter.5.cloned.1.call-done = f32[40,640]{1,0:T(8,128)} async-done(((f32[2560,640]{1,0:T(8,128)}), f32[40,640]{1,0:T(8,128)}) %reduce-scatter.5.cloned.1.call-update) | async-done | bytes 102416
  (87 shorter events, 34.2 us)
Async XLA Ops:
  7.2 5.9 copy-start
  7.2 40.5 %all-gather.15.cloned.1.call-start = ((), (), s32[]{:S(2)}) async-start(), calls=%async_computation.7 | async-start | bytes 3276800 | tf_op jit(solution)/shard_map/all_gather | solution.py:39
  9.6 3.3 copy-start.7
  10.0 3.4 copy-start.8
  12.2 316.7 %all-gather.7.cloned.1.call-start = ((), (), s32[]{:S(2)}) async-start(), calls=%async_computation.3 | async-start | bytes 3328000 | tf_op jit(solution)/shard_map/all_gather | solution.py:81
  13.5 6.6 slice-start
  339.4 6.0 copy-start.6
  340.4 16.1 %all-to-all-start = ((bf16[4,2,40960]{2,1,0:T(2,128)(2,1)}), bf16[4,2,40960]{2,1,0:T(2,128)(2,1)S(1)}, u32[]{:S(2)}, u32[]{:S(2)}) async-start(bf16[4,2,40960]{2,1,0:T(2,128)(2,1)} %reshape.192), calls=%async_computation | async-start | bytes 1310720 | tf_op jit(solution)/shard_map/all_to_all | solution.py:43
  344.8 87.4 %all-gather.9.cloned.1.call-start = ((), (), s32[]{:S(2)}) async-start(), calls=%async_computation.4 | async-start | bytes 6553600 | tf_op jit(solution)/shard_map/all_gather | solution.py:39
  345.7 16.3 %copy-start.2 = (bf16[128,2560]{0,1:T(8,128)(2,1)}, bf16[128,2560]{0,1:T(8,128)(2,1)S(1)}, u32[]{:S(2)}) copy-start(bf16[128,2560]{0,1:T(8,128)(2,1)S(1)} %copy.39) | copy-start | bytes 1966084
  366.8 346.4 %all-gather.11.cloned.1.call-start = ((), (), s32[]{:S(2)}) async-start(), calls=%async_computation.5 | async-start | bytes 3328000 | tf_op jit(solution)/shard_map/all_gather | solution.py:82
  367.4 647.4 %all-gather.13.cloned.1.call-start = ((), (), s32[]{:S(2)}) async-start(), calls=%async_computation.6 | async-start | bytes 3328000 | tf_op jit(solution)/shard_map/all_gather | solution.py:83
  368.0 1088.9 %reduce-scatter.5.cloned.1.call-start = ((), (), s32[]{:S(2)}) async-start(), calls=%async_computation.8 | async-start | bytes 6656000
  718.1 0.8 copy-start.3
  1019.7 0.8 copy-start.4
  1163.1 295.3 %copy-start.1 = (f32[3,8,640]{2,1,0:T(8,128)S(1)}, f32[3,8,640]{2,1,0:T(8,128)}, u32[]{:S(2)}) copy-start(f32[3,8,640]{2,1,0:T(8,128)} %param.17) | copy-start | bytes 184324
  1164.7 1.1 copy-start.5
Sparse Core Ops, SparseCore 0:
  12.3 35.3 all-gather.14
  49.5 279.3 all-gather.6
  366.9 65.1 all-gather.8
  433.8 279.3 all-gather.10
  714.8 299.9 all-gather.12
  1161.0 295.9 reduce-scatter.4
where the time goes:
time: 1490 us; the launch traced here: 1470 us
  waiting for transfers between devices  1230 us (83%)
  blocking collectives  120 us (8%)
  local copies, waits for them, and re-layouts  37.1 us (2%)
  other arithmetic  28.2 us (2%)
  matrix products  27.3 us (2%)
  between operations  15.2 us (1%)
    unnamed x7, waiting for transfers between devices  292 us
    all_gather x1, waiting for transfers between devices, on_device(): lax.all_gather(critic_codes, 'fsdp', axis=0, tiled=True)  290 us
    all_gather x1, waiting for transfers between devices, on_device(): lax.all_gather(gen_codes, 'fsdp', axis=0, tiled=True)  278 us
    all_gather x1, waiting for transfers between devices, on_device(): lax.all_gather(teacher_codes, 'fsdp', axis=0, tiled=True)  271 us
    psum x1, blocking collectives, on_device(): totals = lax.psum(clip_pick * partial_value, ('dp', 'fsdp'))  96.6 us
    all_gather x2, waiting for transfers between devices, gather_group(): return lax.all_gather(stacked, 'dp', axis=1, tiled=True)  91.5 us
  transfers between devices with their start and end apart: 7, of which 7 were waited for; matrix products, arithmetic and copies ran while one was open for 3% of the time, Pallas kernels for 0%

commit v1 on v0

v1 whole, which is shorter than its diff:
```python
import math

import jax
import jax.numpy as jnp
from jax import lax
from jax.experimental import pallas as pl
from jax.experimental.pallas import tpu as pltpu
from jax.sharding import PartitionSpec as P

RMS_EPS = 1e-06
SPREAD_EPS = 1e-05
F32 = jnp.float32
BF16 = jnp.bfloat16
MESH_ID = pl.DeviceIdType.MESH

NY, NZ = 4, 8
D = 2560
COLS = 640
ROWS = 128
GROUP = 4 * ROWS
HALF = 40
PAD = 48
BLK = 80
CA = 256
CB = COLS - CA
CUT = 48
TOKENS = 32768
CLIP_ELEMENTS = 16384 * 2560
TPC = 640
PIECES = 9


def time_features(timesteps, freq_count):
    freq_index = jnp.arange(freq_count, dtype=F32)
    frequency = jnp.exp(freq_index * (-math.log(10000.0) / freq_count))
    phase_angle = timesteps.astype(F32)[:, None] * frequency[None, :]
    return jnp.concatenate([jnp.cos(phase_angle), jnp.sin(phase_angle)], axis=1)


def scratch_table():
    vmem, dma = pltpu.VMEM, pltpu.SemaphoreType.DMA
    return {
        "W": vmem((3, NY, NZ, BLK, COLS), BF16),
        "XO": vmem((3, PAD, COLS), BF16),
        "XS": vmem((3, 2, PAD, COLS), BF16),
        "XG": vmem((4, ROWS, D), BF16),
        "H": vmem((4, GROUP, COLS), BF16),
        "NS": vmem((4, ROWS, COLS), BF16),
        "CL": vmem((GROUP, COLS), F32),
        "NF": vmem((GROUP, COLS), F32),
        "NG": vmem((4, GROUP, COLS), BF16),
        "JH": vmem((2, 4, GROUP, COLS), BF16),
        "ACC": vmem((GROUP, COLS), F32),
        "RP": vmem((GROUP, COLS), BF16),
        "GP": vmem((GROUP, COLS), F32),
        "CT": vmem((GROUP, COLS), BF16),
        "SB": vmem((GROUP, COLS), BF16),
        "DB": vmem((GROUP, COLS), BF16),
        "G": vmem((NY, NZ, BLK, COLS), F32),
        "ZS": vmem((2, 4, NY, BLK, CA), BF16),
        "ZR": vmem((2, 4, NY, BLK, CA), BF16),
        "YS": vmem((2, 2, NZ, BLK, CB), BF16),
        "YR": vmem((2, 2, NZ, BLK, CB), BF16),
        "ys": vmem((2, 2, BLK, CA), BF16),
        "yr": vmem((2, 2, BLK, CA), BF16),
        "zs": vmem((2, 4, BLK, CB), BF16),
        "zr": vmem((2, 4, BLK, CB), BF16),
        "SC": vmem((3, 8, COLS), F32),
        "PK": vmem((8, COLS), F32),
        "TP": vmem((2, 2 * ROWS, TPC), BF16),
        "JM": vmem((2, 2, 4, 1, COLS), F32),
        "SP": vmem((8, 128), F32),
        "SV": vmem((8, 128), F32),
        "SPG": vmem((4, 8, 128), F32),
        "SPZ": vmem((NZ, 8, 128), F32),
        "SPY": vmem((NY, 8, 128), F32),
        "GF": vmem((2, HALF, COLS), F32),
        "OW": vmem((2, HALF, COLS), F32),
        "ag_s": dma((3, 24)),
        "ag_r": dma((3, 24)),
        "x_s": dma((3, 2)),
        "x_r": dma((3, 2)),
        "tk_s": dma((4,)),
        "tk_r": dma((4,)),
        "ns_s": dma((4,)),
        "ns_r": dma((4,)),
        "ng_s": dma((2, 3)),
        "ng_r": dma((2, 3)),
        "sm_s": dma((4,)),
        "sm_r": dma((4,)),
        "dm_s": dma((4,)),
        "dm_r": dma((4,)),
        "sc_s": dma((1,)),
        "sc_r": dma((1,)),
        "tp_m": dma((2,)),
        "sg_s": dma((4,)),
        "sg_r": dma((4,)),
        "sz_s": dma((NZ,)),
        "sz_r": dma((NZ,)),
        "sy_s": dma((NY,)),
        "sy_r": dma((NY,)),
        "rs_s": dma((24,)),
        "rs_r": dma((24,)),
        "ow_s": dma((2,)),
        "ow_r": dma((2,)),
    }


NAMES = tuple(scratch_table())


def kernel(gi, noise, dstep, sgroup, wg, wt, wc, scales, mod, feats, tproj, out_s, out_d, out_w, *rest):
    S = dict(zip(NAMES, rest))
    dp, fs = lax.axis_index("dp"), lax.axis_index("fsdp")
    h, c = dp // 2, dp % 2
    l, plane = fs % 2, fs // 2
    y, z = plane // NZ, plane % NZ
    oh, oc, ol = 1 - h, 1 - c, 1 - l
    q = 2 * l + c
    cb = 2 * ((h + l) % 2) + c

    def dev(h_, c_, y_, z_, l_):
        return (2 * h_ + c_, (y_ * NZ + z_) * 2 + l_)

    def yy(step):
        return (y + step + NY) % NY

    def zz(step):
        return (z + step + NZ) % NZ

    started = []

    def remote(src, dst, ss, rs, target):
        return pltpu.make_async_remote_copy(
            src_ref=src, dst_ref=dst, send_sem=ss, recv_sem=rs, device_id=target, device_id_type=MESH_ID
        )

    def send(src, dst, ss, rs, target):
        copy = remote(src, dst, ss, rs, target)
        copy.start()
        started.append(copy)

    def arrived(dst, ss, rs):
        remote(dst, dst, ss, rs, dev(h, oc, y, z, l)).wait_recv()

    greeted = [dev(h, oc, y, z, l), dev(h, oc, y, z, ol)]
    greeted += [dev(h, c, y, z, ol), dev(oh, c, y, z, l), dev(oh, c, y, z, ol)]
    greeted += [dev(h, c, yy(j), z, l) for j in range(1, NY)]
    greeted += [dev(h, c, y, zz(j), l) for j in range(1, NZ)]
    barrier = pltpu.get_barrier_semaphore()
    for target in greeted:
        pl.semaphore_signal(barrier, inc=1, device_id=target, device_id_type=MESH_ID)
    pl.semaphore_wait(barrier, len(greeted))

    def ag_regions(m, chain, step, way):
        W, s = S["W"], 1 if way == 0 else -1
        if chain == 0:
            lanes = pl.ds(0, CA)
            if step == 0:
                return W.at[m, y, z, :, lanes], W.at[m, yy(-s), z, :, lanes], dev(h, c, yy(s), z, l)
            if step == 1:
                part = pl.ds(way * (CA // 2), CA // 2)
                return W.at[m, yy(-s), z, :, part], W.at[m, yy(2), z, :, part], dev(h, c, yy(s), z, l)
            k = step - 1
            some = pl.ds(0, NY) if k < 4 else pl.ds(way * 2, 2)
            return W.at[m, some, zz(-s * (k - 1)), :, lanes], W.at[m, some, zz(-s * k), :, lanes], dev(h, c, y, zz(s), l)
        lanes = pl.ds(CA, CB)
        if step < 4:
            k = step + 1
            some = pl.ds(0, BLK) if k < 4 else (pl.ds(0, CUT), pl.ds(CUT, BLK - CUT))[way]
            return W.at[m, y, zz(-s * (k - 1)), some, lanes], W.at[m, y, zz(-s * k), some, lanes], dev(h, c, y, zz(s), l)
        if step == 4:
            return W.at[m, y, :, :, lanes], W.at[m, yy(-s), :, :, lanes], dev(h, c, yy(s), z, l)
        some = pl.ds(way * 4, 4)
        return W.at[m, yy(-s), some, :, lanes], W.at[m, yy(2), some, :, lanes], dev(h, c, yy(s), z, l)

    def ag_start(m, chain, step):
        for way in range(2):
            src, _, target = ag_regions(m, chain, step, way)
            i = (chain * 6 + step) * 2 + way
            send(src, src, S["ag_s"].at[m, i], S["ag_r"].at[m, i], target)

    def ag_wait(m, chain, step):
        for way in range(2):
            _, dst, _ = ag_regions(m, chain, step, way)
            i = (chain * 6 + step) * 2 + way
            arrived(dst, S["ag_s"].at[m, i], S["ag_r"].at[m, i])

    XO, XS = S["XO"], S["XS"]

    def x_second(m):
        return remote(XO.at[m], XS.at[m, 1], S["x_s"].at[m, 1], S["x_r"].at[m, 1], dev(h, c, y, z, 0))

    def x_first(m, slot):
        return remote(XO.at[m], XS.at[m, slot], S["x_s"].at[m, 0], S["x_r"].at[m, slot], dev(oh, c, y, z, 1))

    for m, codes in enumerate((wg, wt, wc)):
        own = codes[...].astype(F32)
        own = jnp.concatenate([own, jnp.zeros((PAD - HALF, COLS), F32)], axis=0).astype(BF16)
        XO[m] = own

        @pl.when(l == 0)
        def _():
            XS[m, 0] = own
            x_first(m, 0).start()

        @pl.when(l == 1)
        def _():
            x_second(m).start()
            x_first(m, 1).start()

    def assemble(m):
        @pl.when(l == 1)
        def _():
            arrived(XS.at[m, 0], S["x_s"].at[m, 0], S["x_r"].at[m, 0])

        arrived(XS.at[m, 1], S["x_s"].at[m, 1], S["x_r"].at[m, 1])
        both = [XS[m, i].astype(F32)[:HALF] for i in range(2)]
        S["W"][m, y, z] = jnp.concatenate(both, axis=0).astype(BF16)

    XG, NS, SC = S["XG"], S["NS"], S["SC"]
    send(gi, XG.at[q], S["tk_s"].at[0], S["tk_r"].at[0], dev(h, c, y, z, ol))
    send(gi, XG.at[q], S["tk_s"].at[1], S["tk_r"].at[1], dev(h, oc, y, z, l))
    tok_own = pltpu.make_async_copy(gi, XG.at[q], S["tk_s"].at[3])
    tok_own.start()

    def columns(c_, l_):
        return pl.ds(pl.multiple_of((2 * ((h + l_) % 2) + c_) * COLS, COLS), COLS)

    others = ((oc, l), (c, ol), (oc, ol))
    for i, (c_, l_) in enumerate(others):
        send(noise.at[:, columns(c_, l_)], NS.at[q], S["ns_s"].at[i], S["ns_r"].at[i], dev(h, c_, y, z, l_))
    noise_own = pltpu.make_async_copy(noise.at[:, columns(c, l)], NS.at[q], S["ns_s"].at[3])
    noise_own.start()

    def scale_copy():
        return remote(scales, SC, S["sc_s"].at[0], S["sc_r"].at[0], dev(oh, c, y, z, 1))

    def scale_own():
        return pltpu.make_async_copy(scales, SC, S["sc_r"].at[0])

    @pl.when(l == 0)
    def _():
        scale_copy().start()
        scale_own().start()

    def piece(i):
        m, j = i // PIECES, i % PIECES
        if j < 8:
            offset = j * COLS
        else:
            offset = pl.multiple_of(2 * D + cb * COLS, COLS)
        return pltpu.make_async_copy(tproj.at[m, :, pl.ds(offset, TPC)], S["TP"].at[i % 2], S["tp_m"].at[i % 2])

    piece(0).start()
    piece(1).start()

    def gen_hat(block):
        H = S["H"]

        def rows(r, carry):
            at = pl.ds(pl.multiple_of(r * 16, 16), 16)
            x = XG[block, at, :].astype(F32)
            inv = lax.rsqrt(jnp.sum(x * x, axis=1, keepdims=True) / D + RMS_EPS)
            hat = (x * inv * (1.0 + mod[0, 1:2, :]) + mod[0, 0:1, :]).astype(BF16)
            to = pl.ds(pl.multiple_of(block * ROWS + r * 16, 16), 16)
            for k in range(4):
                H[k, to, :] = hat[:, k * COLS : (k + 1) * COLS]
            return carry

        lax.fori_loop(0, ROWS // 16, rows, 0)

    def judge_mod():
        feature = jnp.where(h == 0, feats[0:1, :], feats[1:2, :])
        hi = feature.astype(BF16)
        rest1 = feature - hi.astype(F32)
        mid = rest1.astype(BF16)
        low = (rest1 - mid.astype(F32)).astype(BF16)
        row = lax.broadcasted_iota(jnp.int32, (16, 2 * ROWS), 0)
        spread_out = [jnp.broadcast_to(v.astype(F32), (16, 2 * ROWS)) for v in (hi, mid, low)]
        parts = jnp.where(row == 0, spread_out[0], jnp.where(row == 1, spread_out[1], jnp.where(row == 2, spread_out[2], 0.0)))
        parts = parts.astype(BF16)
        for i in range(2 * PIECES):
            m, j = i // PIECES, i % PIECES
            piece(i).wait()
            lifted = jnp.dot(parts, S["TP"][i % 2], preferred_element_type=F32)
            lifted = jnp.sum(lifted, axis=0, keepdims=True)
            if j < 8:
                S["JM"][m, j // 4, j % 4] = lifted + mod[m + 1, j // 4 : j // 4 + 1, (j % 4) * COLS : (j % 4 + 1) * COLS]
            else:
                gate = mod[m + 1, 2:3, pl.ds(pl.multiple_of(cb * COLS, COLS), COLS)]
                S["PK"][m + 4 : m + 5, :] = lifted + gate
            if i + 2 < 2 * PIECES:
                piece(i + 2).start()

    def factors():
        arrived(SC, S["sc_s"].at[0], S["sc_r"].at[0])
        row = lax.broadcasted_iota(jnp.int32, (8, COLS), 0)
        for m in range(3):
            picked = jnp.sum(jnp.where(row == sgroup[m, h], SC[m], 0.0), axis=0, keepdims=True)
            if m == 0:
                gate = mod[0, 2:3, pl.ds(pl.multiple_of(cb * COLS, COLS), COLS)]
            else:
                gate = S["PK"][m + 3 : m + 4, :]
            S["PK"][m : m + 1, :] = gate * picked

    def level():
        return jnp.full((1, COLS), dstep[h], jnp.int32).astype(F32) / 1000.0

    def product(lhs, m):
        ACC = S["ACC"]
        for k in range(4):
            part = jnp.dot(lhs[k], S["W"][m, k].reshape(COLS, COLS), preferred_element_type=F32)
            if k == 0:
                ACC[...] = part
            else:
                ACC[...] += part

    TILE = 64

    def clean_rows(half):
        lev = level()
        here = pl.ds(pl.multiple_of(cb * COLS, COLS), COLS)

        def rows(r, carry):
            at = pl.ds(pl.multiple_of(half * (GROUP // 2) + r * TILE, TILE), TILE)
            block = half * 2 + r // 2
            inner = pl.ds(pl.multiple_of((r % 2) * TILE, TILE), TILE)
            branch = (S["ACC"][at, :] * S["PK"][0:1, :]).astype(BF16)
            clean = XG[block, inner, here].astype(F32) + branch.astype(F32)
            noisy = (1.0 - lev) * clean + lev * NS[block, inner, :].astype(F32)
            S["CL"][at, :] = clean
            S["NF"][at, :] = noisy
            S["SB"][at, :] = clean.astype(BF16)
            S["NG"][cb, at, :] = noisy.astype(BF16)
            return carry

        lax.fori_loop(0, GROUP // 2 // TILE, rows, 0)

    def half_rows(half):
        return pl.ds(half * (GROUP // 2), GROUP // 2)

    def noisy_send(half):
        own = S["NG"].at[cb, half_rows(half)]
        send(own, own, S["ng_s"].at[half, 0], S["ng_r"].at[half, 0], dev(h, c, y, z, ol))
        send(own, own, S["ng_s"].at[half, 1], S["ng_r"].at[half, 1], dev(h, oc, y, z, l))

    far = 2 * ((h + ol) % 2) + c

    def noisy_forward(half):
        got = S["NG"].at[far, half_rows(half)]
        arrived(got, S["ng_s"].at[half, 0], S["ng_r"].at[half, 0])
        send(got, got, S["ng_s"].at[half, 2], S["ng_r"].at[half, 2], dev(h, oc, y, z, l))

    def noisy_wait(half):
        near = 2 * ((h + l) % 2) + oc
        last = 2 * ((h + ol) % 2) + oc
        arrived(S["NG"].at[near, half_rows(half)], S["ng_s"].at[half, 1], S["ng_r"].at[half, 1])
        arrived(S["NG"].at[last, half_rows(half)], S["ng_s"].at[half, 2], S["ng_r"].at[half, 2])

    def judge_hats(half):
        NG, JH, JM = S["NG"], S["JH"], S["JM"]

        def rows(r, carry):
            at = pl.ds(pl.multiple_of(half * (GROUP // 2) + r * 16, 16), 16)
            v = [NG[k, at, :].astype(F32) for k in range(4)]
            total = sum(jnp.sum(t * t, axis=1, keepdims=True) for t in v)
            inv = lax.rsqrt(total / D + RMS_EPS)
            for k in range(4):
                normed = (v[k] * inv).astype(BF16).astype(F32)
                for j in range(2):
                    JH[j, k, at, :] = (normed * (1.0 + JM[j, 1, k]) + JM[j, 0, k]).astype(BF16)
            return carry

        lax.fori_loop(0, GROUP // 2 // 16, rows, 0)

    def return_rows(buf, out, ss, rs):
        here = pl.ds(pl.multiple_of(cb * COLS, COLS), COLS)
        for i, (c_, l_) in enumerate(others):
            block = pl.ds(pl.multiple_of((2 * l_ + c_) * ROWS, ROWS), ROWS)
            send(buf.at[block], out.at[:, here], ss.at[i], rs.at[i], dev(h, c_, y, z, l_))
        block = pl.ds(pl.multiple_of(q * ROWS, ROWS), ROWS)
        own = pltpu.make_async_copy(buf.at[block], out.at[:, here], ss.at[3])
        own.start()
        return own

    def return_wait(out, ss, rs):
        for i, (c_, l_) in enumerate(others):
            arrived(out.at[:, columns(c_, l_)], ss.at[i], rs.at[i])

    def real_rows():
        def rows(r, carry):
            at = pl.ds(pl.multiple_of(r * TILE, TILE), TILE)
            S["RP"][at, :] = (S["ACC"][at, :] * S["PK"][1:2, :]).astype(BF16)
            return carry

        lax.fori_loop(0, GROUP // TILE, rows, 0)

    def spread_rows():
        lev = level()

        def rows(r, total):
            at = pl.ds(pl.multiple_of(r * TILE, TILE), TILE)
            noisy = S["NF"][at, :]
            gone = jnp.abs(S["CL"][at, :] - (noisy - lev * (noisy + S["RP"][at, :].astype(F32))))
            return total + jnp.sum(gone.reshape(TILE // 8, 8, COLS), axis=0)

        total = lax.fori_loop(0, GROUP // TILE, rows, jnp.zeros((8, COLS), F32))
        total = jnp.sum(jnp.sum(total, axis=1, keepdims=True), axis=0, keepdims=True)
        S["SP"][...] = jnp.broadcast_to(total, (8, 128))

    def gap_rows():
        lev = level()

        def rows(r, carry):
            at = pl.ds(pl.multiple_of(r * TILE, TILE), TILE)
            fake = (S["ACC"][at, :] * S["PK"][2:3, :]).astype(BF16).astype(F32)
            gap = lev * (S["RP"][at, :].astype(F32) - fake)
            S["GP"][at, :] = gap
            S["CT"][at, :] = (gap * S["PK"][0:1, :]).astype(BF16)
            return carry

        lax.fori_loop(0, GROUP // TILE, rows, 0)

    def spread_group_start():
        S["SPG"][q] = S["SP"][...]
        for i, (c_, l_) in enumerate(others):
            send(S["SP"], S["SPG"].at[q], S["sg_s"].at[i], S["sg_r"].at[i], dev(h, c_, y, z, l_))

    def spread_z_start():
        for i, (c_, l_) in enumerate(others):
            arrived(S["SPG"].at[2 * l_ + c_], S["sg_s"].at[i], S["sg_r"].at[i])
        SPG, SPZ = S["SPG"], S["SPZ"]
        SPZ[z] = (SPG[0] + SPG[1]) + (SPG[2] + SPG[3])
        for j in range(1, NZ):
            send(SPZ.at[z], SPZ.at[z], S["sz_s"].at[j], S["sz_r"].at[j], dev(h, c, y, zz(j), l))

    def spread_y_start():
        SPZ, SPY = S["SPZ"], S["SPY"]
        for j in range(1, NZ):
            arrived(SPZ.at[zz(-j)], S["sz_s"].at[j], S["sz_r"].at[j])
        total = SPZ[0]
        for j in range(1, NZ):
            total = total + SPZ[j]
        SPY[y] = total
        for j in range(1, NY):
            send(SPY.at[y], SPY.at[y], S["sy_s"].at[j], S["sy_r"].at[j], dev(h, c, yy(j), z, l))

    def spread_value():
        SPY = S["SPY"]
        for j in range(1, NY):
            arrived(SPY.at[yy(-j)], S["sy_s"].at[j], S["sy_r"].at[j])
        total = SPY[0]
        for j in range(1, NY):
            total = total + SPY[j]
        S["SV"][...] = total / CLIP_ELEMENTS + SPREAD_EPS

    def dmd_rows():
        def rows(r, carry):
            at = pl.ds(pl.multiple_of(r * TILE, TILE), TILE)
            S["DB"][at, :] = (S["GP"][at, :] / S["SV"][0:1, 0:1]).astype(BF16)
            return carry

        lax.fori_loop(0, GROUP // TILE, rows, 0)

    G = S["G"]

    def grad(k):
        block = lax.dot_general(S["H"][k], S["CT"][...], (((0,), (0,)), ((), ())), preferred_element_type=F32)
        G[k] = block.reshape(NZ, BLK, COLS)

    def rs_send(i, src, dst, target):
        send(src, dst, S["rs_s"].at[i], S["rs_r"].at[i], target)

    def rs_got(i, dst):
        arrived(dst, S["rs_s"].at[i], S["rs_r"].at[i])

    LB = pl.ds(CA, CB)
    LA = pl.ds(0, CA)

    def big_y(step):
        YS, YR = S["YS"], S["YR"]
        for way in range(2):
            s = 1 if way == 0 else -1
            some = pl.ds(way * 4, 4)
            if step == 0:
                for i in range(way * 4, way * 4 + 4):
                    YS[way, 0, i] = G[yy(2), i, :, LB].astype(BF16)
                rs_send(way, YS.at[way, 0, some], YR.at[way, 0, some], dev(h, c, yy(s), z, l))
            else:
                rs_got(way, YR.at[way, 0, some])
                for i in range(NZ):
                    v = G[yy(s), i, :, LB]
                    if way * 4 <= i < way * 4 + 4:
                        v = v + YR[way, 0, i].astype(F32)
                    YS[way, 1, i] = v.astype(BF16)
                rs_send(2 + way, YS.at[way, 1], YR.at[way, 1], dev(h, c, yy(s), z, l))

    def big_y_end():
        YR = S["YR"]
        for way in range(2):
            rs_got(2 + way, YR.at[way, 1])
        for i in range(NZ):
            G[y, i, :, LB] = G[y, i, :, LB] + YR[0, 1, i].astype(F32) + YR[1, 1, i].astype(F32)

    def big_z(k):
        ZS, ZR = S["ZS"], S["ZR"]
        for way in range(2):
            s = 1 if way == 0 else -1
            half = range(way * 2, way * 2 + 2)
            some = pl.ds(way * 2, 2)
            if k > 1:
                got = ZR.at[way, k - 2, some] if k == 2 else ZR.at[way, k - 2]
                rs_got(4 + 2 * (k - 2) + way, got)
            if k < 5:
                for i in half if k == 1 else range(NY):
                    v = G[i, zz(s * (5 - k)), :, LA]
                    if k > 2 or (k == 2 and i in half):
                        v = v + ZR[way, k - 2, i].astype(F32)
                    ZS[way, k - 1, i] = v.astype(BF16)
                src = ZS.at[way, k - 1, some] if k == 1 else ZS.at[way, k - 1]
                dst = ZR.at[way, k - 1, some] if k == 1 else ZR.at[way, k - 1]
                rs_send(4 + 2 * (k - 1) + way, src, dst, dev(h, c, y, zz(s), l))
        if k == 5:
            for i in range(NY):
                G[i, z, :, LA] = G[i, z, :, LA] + ZR[0, 3, i].astype(F32) + ZR[1, 3, i].astype(F32)

    def small_y(step):
        ys, yr = S["ys"], S["yr"]
        for way in range(2):
            s = 1 if way == 0 else -1
            part = pl.ds(way * (CA // 2), CA // 2)
            if step == 0:
                ys[way, 0, :, part] = G[yy(2), z, :, part].astype(BF16)
                rs_send(12 + way, ys.at[way, 0, :, part], yr.at[way, 0, :, part], dev(h, c, yy(s), z, l))
            elif step == 1:
                rs_got(12 + way, yr.at[way, 0, :, part])
                ys[way, 1] = G[yy(s), z, :, LA].astype(BF16)
                ys[way, 1, :, part] = (G[yy(s), z, :, part] + yr[way, 0, :, part].astype(F32)).astype(BF16)
                rs_send(14 + way, ys.at[way, 1], yr.at[way, 1], dev(h, c, yy(s), z, l))
            else:
                rs_got(14 + way, yr.at[way, 1])
        if step == 2:
            G[y, z, :, LA] = G[y, z, :, LA] + yr[0, 1].astype(F32) + yr[1, 1].astype(F32)

    def small_z(k):
        zs, zr = S["zs"], S["zr"]
        for way in range(2):
            s = 1 if way == 0 else -1
            some = (pl.ds(0, CUT), pl.ds(CUT, BLK - CUT))[way]
            if k > 1:
                got = zr.at[way, 0, some] if k == 2 else zr.at[way, k - 2]
                rs_got(16 + 2 * (k - 2) + way, got)
            if k == 1:
                zs[way, 0, some, :] = G[y, zz(4 * s), some, LB].astype(BF16)
                rs_send(16 + way, zs.at[way, 0, some], zr.at[way, 0, some], dev(h, c, y, zz(s), l))
            elif k < 5:
                v = G[y, zz(s * (5 - k)), :, LB]
                if k > 2:
                    zs[way, k - 1] = (v + zr[way, k - 2].astype(F32)).astype(BF16)
                else:
                    zs[way, 1] = v.astype(BF16)
                    zs[way, 1, some, :] = (G[y, zz(3 * s), some, LB] + zr[way, 0, some, :].astype(F32)).astype(BF16)
                rs_send(16 + 2 * (k - 1) + way, zs.at[way, k - 1], zr.at[way, k - 1], dev(h, c, y, zz(s), l))
        if k == 5:
            G[y, z, :, LB] = G[y, z, :, LB] + zr[0, 3].astype(F32) + zr[1, 3].astype(F32)

    for m in range(3):
        assemble(m)
        ag_start(m, 0, 0)
        ag_start(m, 1, 0)
    tok_own.wait()
    gen_hat(q)
    for m in range(3):
        ag_wait(m, 0, 0)
        ag_start(m, 0, 1)
        ag_wait(m, 1, 0)
        ag_start(m, 1, 1)
    q_far = 2 * ol + c
    arrived(XG.at[q_far], S["tk_s"].at[0], S["tk_r"].at[0])
    send(XG.at[q_far], XG.at[q_far], S["tk_s"].at[2], S["tk_r"].at[2], dev(h, oc, y, z, l))
    ag_wait(0, 0, 1)
    ag_start(0, 0, 2)
    ag_wait(0, 1, 1)
    ag_start(0, 1, 2)
    for m in (1, 2):
        ag_wait(m, 0, 1)
        ag_wait(m, 1, 1)
        ag_start(m, 1, 2)
    for m in range(3):
        ag_wait(m, 1, 2)
        ag_start(m, 1, 3)
    q_near = 2 * l + oc
    arrived(XG.at[q_near], S["tk_s"].at[1], S["tk_r"].at[1])
    gen_hat(q_near)
    ag_wait(0, 1, 3)
    ag_start(0, 1, 4)
    ag_wait(0, 0, 2)
    ag_start(0, 0, 3)
    ag_start(1, 0, 2)
    gen_hat(q_far)
    for m in (1, 2):
        ag_wait(m, 1, 3)
    ag_wait(0, 0, 3)
    ag_start(0, 0, 4)
    q_last = 2 * ol + oc
    arrived(XG.at[q_last], S["tk_s"].at[2], S["tk_r"].at[2])
    gen_hat(q_last)
    ag_start(1, 1, 4)
    ag_wait(1, 0, 2)
    ag_start(1, 0, 3)
    ag_wait(0, 0, 4)
    ag_start(0, 0, 5)
    ag_wait(0, 1, 4)
    ag_start(0, 1, 5)
    judge_mod()
    factors()
    ag_wait(1, 0, 3)
    ag_start(1, 0, 4)
    ag_start(2, 0, 2)
    ag_wait(0, 0, 5)
    ag_wait(0, 1, 5)
    ag_start(2, 1, 4)
    product(S["H"], 0)
    noise_own.wait()
    for i, (c_, l_) in enumerate(others):
        arrived(NS.at[2 * l_ + c_], S["ns_s"].at[i], S["ns_r"].at[i])
    for half in range(2):
        clean_rows(half)
        noisy_send(half)
    ag_wait(1, 0, 4)
    ag_start(1, 0, 5)
    ag_wait(2, 0, 2)
    ag_start(2, 0, 3)
    ag_wait(1, 1, 4)
    ag_start(1, 1, 5)
    noisy_forward(0)
    ag_wait(2, 0, 3)
    ag_start(2, 0, 4)
    noisy_forward(1)
    ag_wait(1, 0, 5)
    sample_own = return_rows(S["SB"], out_s, S["sm_s"], S["sm_r"])
    noisy_wait(0)
    judge_hats(0)
    ag_wait(2, 0, 4)
    ag_start(2, 0, 5)
    ag_wait(2, 1, 4)
    ag_start(2, 1, 5)
    noisy_wait(1)
    judge_hats(1)
    ag_wait(1, 1, 5)
    product(S["JH"].at[0], 1)
    real_rows()
    spread_rows()
    spread_group_start()
    ag_wait(2, 0, 5)
    ag_wait(2, 1, 5)
    product(S["JH"].at[1], 2)
    gap_rows()
    spread_z_start()
    grad(yy(2))
    big_y(0)
    grad(yy(1))
    grad(yy(-1))
    big_y(1)
    grad(y)
    spread_y_start()
    big_z(1)
    big_z(2)
    spread_value()
    dmd_rows()
    dmd_own = return_rows(S["DB"], out_d, S["dm_s"], S["dm_r"])
    big_z(3)
    big_z(4)
    big_y_end()
    small_z(1)
    big_z(5)
    small_y(0)
    small_z(2)
    small_y(1)
    small_z(3)
    small_y(2)
    small_z(4)
    small_z(5)
    GF, OW = S["GF"], S["OW"]
    done = G[y, z] / S["SV"][0:1, 0:1] / TOKENS

    def own_row(row, slot, target):
        return remote(GF.at[row], OW.at[slot], S["ow_s"].at[row], S["ow_r"].at[slot], target)

    for row in range(2):
        GF[row] = done[row * HALF : (row + 1) * HALF]

    @pl.when(l == 0)
    def _():
        OW[0] = GF[0]
        own_row(1, 0, dev(h, c, y, z, 1)).start()

    @pl.when(l == 1)
    def _():
        own_row(0, 1, dev(oh, c, y, z, 0)).start()
        own_row(1, 1, dev(oh, c, y, z, 1)).start()
        arrived(OW.at[0], S["ow_s"].at[0], S["ow_r"].at[0])

    arrived(OW.at[1], S["ow_s"].at[1], S["ow_r"].at[1])
    out_w[...] = OW[0] + OW[1]

    return_wait(out_s, S["sm_s"], S["sm_r"])
    return_wait(out_d, S["dm_s"], S["dm_r"])
    sample_own.wait()
    dmd_own.wait()
    for copy in started:
        copy.wait_send()
    for m in range(3):
        x_first(m, 0).wait_send()

    @pl.when(l == 0)
    def _():
        scale_copy().wait_send()
        own_row(1, 0, dev(h, c, y, z, 1)).wait_send()

    @pl.when(l == 1)
    def _():
        for m in range(3):
            x_second(m).wait_send()
        own_row(0, 1, dev(oh, c, y, z, 0)).wait_send()
        own_row(1, 1, dev(oh, c, y, z, 1)).wait_send()


def on_device(gi, noise, dmd_step, scale_group, wg, wt, wc, scales, mod, tproj):
    feats = time_features(dmd_step, tproj.shape[1] // 2)
    vmem = pl.BlockSpec(memory_space=pltpu.VMEM)
    smem = pl.BlockSpec(memory_space=pltpu.SMEM)
    hbm = pl.BlockSpec(memory_space=pl.ANY)
    return pl.pallas_call(
        kernel,
        out_shape=(
            jax.ShapeDtypeStruct((ROWS, D), BF16),
            jax.ShapeDtypeStruct((ROWS, D), BF16),
            jax.ShapeDtypeStruct((HALF, COLS), F32),
        ),
        in_specs=[hbm, hbm, smem, smem, vmem, vmem, vmem, hbm, vmem, vmem, hbm],
        out_specs=(hbm, hbm, vmem),
        scratch_shapes=list(scratch_table().values()),
        compiler_params=pltpu.CompilerParams(
            collective_id=0, has_side_effects=True, vmem_limit_bytes=64 * 1024 * 1024 - 65536
        ),
    )(gi, noise, dmd_step, scale_group, wg, wt, wc, scales, mod, feats, tproj)


def solution(mesh):
    return jax.shard_map(
        on_device,
        mesh=mesh,
        in_specs=(
            P(("dp", "fsdp"), None),
            P(("dp", "fsdp"), None),
            P(),
            P(),
            P("fsdp", "dp"),
            P("fsdp", "dp"),
            P("fsdp", "dp"),
            P(None, None, "dp"),
            P(),
            P(),
        ),
        out_specs=(P(("dp", "fsdp"), None), P(("dp", "fsdp"), None), P("fsdp", "dp")),
        check_vma=False,
    )
```

time: 1490 us -> 159 us (0.11); the launches traced: 1470 us -> 158 us
  waiting for transfers between devices: 1230 us -> 0 us
  Pallas kernels: 0 us -> 149 us
  blocking collectives: 120 us -> 0 us
  local copies, waits for them, and re-layouts: 37.1 us -> 6.81 us
  matrix products: 27.3 us -> 0 us
  other arithmetic: 28.2 us -> 1.37 us
    all_gather x5 -> x0, waiting for transfers between devices: 932 us -> none  [the longest x1 290 us: on_device(): lax.all_gather(critic_codes, 'fsdp', axis=0, tiled=True)]
    unnamed x7 -> x0, waiting for transfers between devices: 292 us -> none
    pallas_call x0 -> x1, Pallas kernels: none -> 149 us  [on_device(): pl.pallas_call(kernel, out_shape=(jax.ShapeDtypeStruct((ROWS, D), BF16),...]
    psum x1 -> x0, blocking collectives: 96.6 us -> none  [on_device(): totals = lax.psum(clip_pick * partial_value, ('dp', 'fsdp'))]
    dot_general x6 -> x0, matrix products: 27.3 us -> none  [the longest x1 6.69 us: on_device(): lax.dot_general(hat_group, cotangent, (((0,), (0,)), ((), ())), preferred...]
    all_to_all x1 -> x0, blocking collectives: 23 us -> none  [return_tokens(): lax.all_to_all(stacked, 'dp', split_axis=1, concat_axis=2, tiled=True)]
  transfers between devices with their start and end apart: 7 -> 0, of which waited for: 7 -> 0; matrix products, arithmetic and copies ran while one was open for 3% -> 0% of each run, Pallas kernels for 0% -> 0%
where the time goes in v1:
time: 159 us; the launch traced here: 158 us
  Pallas kernels  149 us (94%)
  local copies, waits for them, and re-layouts  6.81 us (4%)
    pallas_call x1, Pallas kernels, on_device(): pl.pallas_call(kernel, out_shape=(jax.ShapeDtypeStruct((ROWS, D), BF16),...  149 us
    unnamed x4, local copies, waits for them, and re-layouts  6.81 us

profile of v1, /device:TPU:8, one launch (start us, length us, event | category | flops | bytes accessed | tf_op | source)
XLA Modules:
  0.0 158.0 jit_solution(11349032249668829727)
XLA Ops:
  0.6 0.7 convert_element_type.3
  1.3 0.1 multiply_cosine_fusion
  1.4 0.6 pad_maximum_fusion.feats
  2.0 1.3 copy.13.sgroup
  3.3 149.2 %shard_map.121 = (bf16[128,2560]{1,0:T(8,128)(2,1)}, bf16[128,2560]{1,0:T(8,128)(2,1)}, f32[40,640]{1,0:T(8,128)}) custom-call(bf16[128,2560]{1,0:T(8,128)(2,1)} %gi.1, bf16[128,2560]{1,0:T(8,128)(2,1)} %noise.1, s32[2]{0:T(128)} %dstep.1, s32[3,2]{1,0:T(4,128)} %copy.13.sgroup, bf16[40,640]{1,0:T(8,128)(2,1)} %wg.1, bf16[40,640]{1,0:T(8,128)(2,1)} %wt.1, ...), custom_call_target="tpu_custom_call" | custom-call | tf_op jit(solution)/shard_map/pallas_call | solution.py:735
  152.5 2.0 %copy.17 = bf16[128,2560]{1,0:T(8,128)(2,1)} copy(bf16[128,2560]{1,0:T(8,128)(2,1)} %get-tuple-element.8) | data formatting | bytes 1310720
  154.5 2.0 %copy.18 = bf16[128,2560]{1,0:T(8,128)(2,1)} copy(bf16[128,2560]{1,0:T(8,128)(2,1)} %get-tuple-element.9) | data formatting | bytes 1310720
  156.5 1.5 copy.19
  (1 shorter events, 0.0 us)

commit v2 on v0

v2 whole, which is shorter than its diff:
```python
import functools
import math
import types

import jax
import jax.numpy as jnp
from jax import lax
from jax.experimental import pallas as pl
from jax.experimental.pallas import tpu as pltpu
from jax.sharding import PartitionSpec as P

RMS_EPS = 1e-06
SPREAD_EPS = 1e-05
F32 = jnp.float32
BF16 = jnp.bfloat16
MESH_ID = pl.DeviceIdType.MESH

NY, NZ = 4, 8
D = 2560
COLS = 640
ROWS = 128
GROUP = 4 * ROWS
HALF = 40
PAD = 48
BLK = 80
CA = 256
CB = COLS - CA
CUT = 48
TOKENS = 32768
CLIP_ELEMENTS = 16384 * 2560
TPC = 640
PIECES = 9
SLOTS = 4
AY, AZ, BZ, BY, FY = range(5)


def scratch_table():
    vmem, dma = pltpu.VMEM, pltpu.SemaphoreType.DMA
    return dict(
        W=vmem((3, NY, NZ, BLK, COLS), BF16),
        XO=vmem((3, PAD, COLS), BF16),
        XS=vmem((3, 2, PAD, COLS), BF16),
        XG=vmem((4, ROWS, D), BF16),
        H=vmem((4, GROUP, COLS), BF16),
        NS=vmem((4, ROWS, COLS), BF16),
        CL=vmem((GROUP, COLS), F32),
        NF=vmem((GROUP, COLS), F32),
        NG=vmem((4, GROUP, COLS), BF16),
        JH=vmem((2, 4, GROUP, COLS), BF16),
        ACC=vmem((GROUP, COLS), F32),
        RP=vmem((GROUP, COLS), BF16),
        GP=vmem((GROUP, COLS), F32),
        CT=vmem((GROUP, COLS), BF16),
        SB=vmem((GROUP, COLS), BF16),
        DB=vmem((GROUP, COLS), BF16),
        G=vmem((NY, NZ, BLK, COLS), F32),
        ZS=vmem((8, NY, BLK, CA), BF16),
        ZR=vmem((8, NY, BLK, CA), BF16),
        Y0S=vmem((NZ, BLK, CB), BF16),
        Y0R=vmem((NZ, BLK, CB), BF16),
        Y1S=vmem((NZ, 2, BLK, CB), BF16),
        Y1R=vmem((NZ, 2, BLK, CB), BF16),
        ys=vmem((4, BLK, CA), BF16),
        yr=vmem((4, BLK, CA), BF16),
        zs=vmem((8, BLK, CB), BF16),
        zr=vmem((8, BLK, CB), BF16),
        SC=vmem((3, 8, COLS), F32),
        PK=vmem((8, COLS), F32),
        TP=vmem((SLOTS, 2 * ROWS, TPC), BF16),
        FT=vmem((16, 2 * ROWS), BF16),
        JM=vmem((2, 2, 4, 1, COLS), F32),
        SP=vmem((8, 128), F32),
        SV=vmem((8, 128), F32),
        SPG=vmem((4, 8, 128), F32),
        SPZ=vmem((NZ, 8, 128), F32),
        SPY=vmem((NY, 8, 128), F32),
        GF=vmem((2, HALF, COLS), F32),
        OW=vmem((2, HALF, COLS), F32),
        ag_s=dma((3, 4)),
        ag_r=dma((3, 18)),
        fy_r=dma((16,)),
        x_s=dma((3, 2)),
        x_r=dma((3, 2)),
        tk_s=dma((4,)),
        tk_r=dma((4,)),
        ns_s=dma((4,)),
        ns_r=dma((4,)),
        ng_s=dma((4, 3)),
        ng_r=dma((4, 3)),
        sm_s=dma((4,)),
        sm_r=dma((4,)),
        dm_s=dma((4,)),
        dm_r=dma((4,)),
        sc_s=dma((1,)),
        sc_r=dma((1,)),
        tp_m=dma((SLOTS,)),
        sg_s=dma((4,)),
        sg_r=dma((4,)),
        sz_s=dma((NZ,)),
        sz_r=dma((NZ,)),
        sy_s=dma((NY,)),
        sy_r=dma((NY,)),
        rs_s=dma((5,)),
        b0_r=dma((NZ,)),
        b1_r=dma((NZ,)),
        a_r=dma((4, NY)),
        y_r=dma((2,)),
        z_r=dma((4,)),
        ow_s=dma((2,)),
        ow_r=dma((2,)),
    )


NAMES = tuple(scratch_table())


def kernel(gi, noise, dstep, sgroup, wg, wt, wc, scales, mod, tproj, out_s, out_d, out_w, *rest):
    S = types.SimpleNamespace(**dict(zip(NAMES, rest)))
    dp, fs = lax.axis_index("dp"), lax.axis_index("fsdp")
    h, c = dp // 2, dp % 2
    l, plane = fs % 2, fs // 2
    y, z = plane // NZ, plane % NZ
    oh, oc, ol = 1 - h, 1 - c, 1 - l
    q = 2 * l + c
    cb = 2 * ((h + l) % 2) + c

    def dev(h_, c_, y_, z_, l_):
        return (2 * h_ + c_, (y_ * NZ + z_) * 2 + l_)

    def yy(step):
        return (y + step + NY) % NY

    def zz(step):
        return (z + step + NZ) % NZ

    started = []

    def remote(src, dst, ss, rs, target):
        return pltpu.make_async_remote_copy(
            src_ref=src, dst_ref=dst, send_sem=ss, recv_sem=rs, device_id=target, device_id_type=MESH_ID
        )

    def send(src, dst, ss, rs, target):
        copy = remote(src, dst, ss, rs, target)
        copy.start()
        started.append(copy)

    def drain():
        for copy in started:
            copy.wait_send()
        started.clear()

    def arrived(dst, ss, rs):
        remote(dst, dst, ss, rs, dev(h, oc, y, z, l)).wait_recv()

    greeted = [dev(h, oc, y, z, l), dev(h, oc, y, z, ol)]
    greeted += [dev(h, c, y, z, ol), dev(oh, c, y, z, l), dev(oh, c, y, z, ol)]
    greeted += [dev(h, c, yy(j), z, l) for j in range(1, NY)]
    greeted += [dev(h, c, y, zz(j), l) for j in range(1, NZ)]
    barrier = pltpu.get_barrier_semaphore()
    for target in greeted:
        pl.semaphore_signal(barrier, inc=1, device_id=target, device_id_type=MESH_ID)

    LA, LB = pl.ds(0, CA), pl.ds(CA, CB)
    Z_ORDER = (4, 3, 5, 2, 6, 1, 7, 0)
    Y_ORDER = (2, 1, -1, 0)
    way_of = {r: i % 2 for i, r in enumerate(Z_ORDER)}

    def ag_copies(m, op, k, i):
        W = S.W
        for way in range(2):
            s = 1 - 2 * way
            if op == AY:
                if k == 1:
                    yield W.at[m, y, z, :, LA], W.at[m, yy(-s), z, :, LA], way
                else:
                    part = pl.ds(way * (CA // 2), CA // 2)
                    yield W.at[m, yy(-s), z, :, part], W.at[m, yy(2), z, :, part], way
            elif op == AZ:
                if k < 4 or way == i:
                    some = pl.ds(2 * i, 2)
                    yield W.at[m, some, zz(-s * (k - 1)), :, LA], W.at[m, some, zz(-s * k), :, LA], way
            elif op == BZ:
                some = pl.ds(0, BLK) if k < 4 else (pl.ds(0, CUT), pl.ds(CUT, BLK - CUT))[way]
                yield W.at[m, y, zz(-s * (k - 1)), some, LB], W.at[m, y, zz(-s * k), some, LB], way
            else:
                some = pl.ds(4 * i, 4) if op == BY else zz(i)
                if k == 1:
                    yield W.at[m, y, some, :, LB], W.at[m, yy(-s), some, :, LB], way
                elif way == (i if op == BY else way_of[i]):
                    yield W.at[m, yy(-s), some, :, LB], W.at[m, yy(2), some, :, LB], way

    def ag_sems(m, op, k, i):
        n = {AY: k - 1, AZ: 2 + (k - 1) * 2 + i, BZ: 9 + k, BY: 12 + 2 * k + i, FY: 18 + 8 * (k - 1) + i}[op]
        group = {AY: 0, AZ: 1, BZ: 2, BY: 3, FY: 3}[op]
        return S.ag_s.at[m, group], S.fy_r.at[n - 18] if op == FY else S.ag_r.at[m, n]

    def ag_go(m, op, k, i=0):
        ss, rs = ag_sems(m, op, k, i)
        for src, _, way in ag_copies(m, op, k, i):
            s = 1 - 2 * way
            target = dev(h, c, y, zz(s), l) if op in (AZ, BZ) else dev(h, c, yy(s), z, l)
            remote(src, src, ss, rs, target).start()

    def ag_got(m, op, k, i=0):
        W = S.W
        ss, rs = ag_sems(m, op, k, i)
        if op == AY:
            both = W.at[m, 0:2, z, :, LA] if k == 1 else W.at[m, 0, z, :, LA]
        elif op == AZ:
            both = W.at[m, :, z, :, LA] if k < 4 else W.at[m, 0:2, z, :, LA]
        elif op == BZ:
            both = W.at[m, 0, 0:2, :, LB] if k < 4 else W.at[m, 0, 0, :, LB]
        elif op == BY:
            both = W.at[m, 0, :, :, LB] if k == 1 else W.at[m, 0, 0:4, :, LB]
        else:
            both = W.at[m, 0, 0:2, :, LB] if k == 1 else W.at[m, 0, 0, :, LB]
        arrived(both, ss, rs)

    def ag_sent(m):
        W = S.W
        for group, whole in enumerate(
            (W.at[m, 0:3, 0, :, LA], W.at[m, :, 0:7, :, LA], W.at[m, 0, 0:7, :, LB], W.at[m, 0:3, :, :, LB])
        ):
            remote(whole, whole, S.ag_s.at[m, group], S.ag_r.at[m, 0], dev(h, oc, y, z, l)).wait_send()

    XO, XS = S.XO, S.XS

    def x_second(m):
        return remote(XO.at[m], XS.at[m, 1], S.x_s.at[m, 1], S.x_r.at[m, 1], dev(h, c, y, z, 0))

    def x_first(m, slot):
        return remote(XO.at[m], XS.at[m, slot], S.x_s.at[m, 0], S.x_r.at[m, slot], dev(oh, c, y, z, 1))

    def x_prepare():
        for m, codes in enumerate((wg, wt, wc)):
            own = codes[...].astype(F32)
            own = jnp.concatenate([own, jnp.zeros((PAD - HALF, COLS), F32)], axis=0).astype(BF16)
            XO[m] = own

            @pl.when(l == 0)
            def _():
                XS[m, 0] = own

    def x_start(m):
        @pl.when(l == 0)
        def _():
            x_first(m, 0).start()

        @pl.when(l == 1)
        def _():
            x_second(m).start()
            x_first(m, 1).start()

    def assemble(m):
        @pl.when(l == 1)
        def _():
            arrived(XS.at[m, 0], S.x_s.at[m, 0], S.x_r.at[m, 0])

        arrived(XS.at[m, 1], S.x_s.at[m, 1], S.x_r.at[m, 1])
        both = [XS[m, i].astype(F32)[:HALF] for i in range(2)]
        S.W[m, y, z] = jnp.concatenate(both, axis=0).astype(BF16)

    XG, NS, SC = S.XG, S.NS, S.SC
    tok_own = pltpu.make_async_copy(gi, XG.at[q], S.tk_s.at[3])

    def tok_near():
        send(gi, XG.at[q], S.tk_s.at[1], S.tk_r.at[1], dev(h, oc, y, z, l))

    def tok_far():
        send(gi, XG.at[q], S.tk_s.at[0], S.tk_r.at[0], dev(h, c, y, z, ol))

    def tok_forward():
        arrived(XG.at[q_far], S.tk_s.at[0], S.tk_r.at[0])
        send(XG.at[q_far], XG.at[q_far], S.tk_s.at[2], S.tk_r.at[2], dev(h, oc, y, z, l))

    q_far, q_near, q_last = 2 * ol + c, 2 * l + oc, 2 * ol + oc

    def columns(c_, l_):
        return pl.ds(pl.multiple_of((2 * ((h + l_) % 2) + c_) * COLS, COLS), COLS)

    others = ((oc, l), (c, ol), (oc, ol))

    def noise_send(i):
        c_, l_ = others[i]
        send(noise.at[:, columns(c_, l_)], NS.at[q], S.ns_s.at[i], S.ns_r.at[i], dev(h, c_, y, z, l_))

    def noise_wait():
        noise_own.wait()
        for i, (c_, l_) in enumerate(others):
            arrived(NS.at[2 * l_ + c_], S.ns_s.at[i], S.ns_r.at[i])

    noise_own = pltpu.make_async_copy(noise.at[:, columns(c, l)], NS.at[q], S.ns_s.at[3])

    def scale_copy():
        return remote(scales, SC, S.sc_s.at[0], S.sc_r.at[0], dev(oh, c, y, z, 1))

    def scale_own():
        return pltpu.make_async_copy(scales, SC, S.sc_r.at[0])

    def scale_start():
        @pl.when(l == 0)
        def _():
            scale_copy().start()
            scale_own().start()

    def piece(i):
        m, j = i // PIECES, i % PIECES
        if j < 8:
            offset = j * COLS
        else:
            offset = pl.multiple_of(2 * D + cb * COLS, COLS)
        return pltpu.make_async_copy(tproj.at[m, :, pl.ds(offset, TPC)], S.TP.at[i % SLOTS], S.tp_m.at[i % SLOTS])

    def gen_hat(block, part):
        H = S.H

        def rows(r, carry):
            at = pl.ds(pl.multiple_of(part * 32 + r * 16, 16), 16)
            x = XG[block, at, :].astype(F32)
            inv = lax.rsqrt(jnp.sum(x * x, axis=1, keepdims=True) / D + RMS_EPS)
            hat = (x * inv * (1.0 + mod[0, 1:2, :]) + mod[0, 0:1, :]).astype(BF16)
            to = pl.ds(pl.multiple_of(block * ROWS + part * 32 + r * 16, 16), 16)
            for k in range(4):
                H[k, to, :] = hat[:, k * COLS : (k + 1) * COLS]
            return carry

        lax.fori_loop(0, 2, rows, 0)

    def features():
        index = lax.broadcasted_iota(jnp.int32, (1, ROWS), 1).astype(F32)
        frequency = jnp.exp(index * (-math.log(10000.0) / ROWS))
        phase = jnp.full((1, ROWS), dstep[h], jnp.int32).astype(F32) * frequency
        feature = jnp.concatenate([jnp.cos(phase), jnp.sin(phase)], axis=1)
        hi = feature.astype(BF16).astype(F32)
        mid = (feature - hi).astype(BF16).astype(F32)
        low = (feature - hi - mid).astype(BF16).astype(F32)
        row = lax.broadcasted_iota(jnp.int32, (16, 2 * ROWS), 0)
        a, b, d = [jnp.broadcast_to(v, (16, 2 * ROWS)) for v in (hi, mid, low)]
        S.FT[...] = jnp.where(row == 0, a, jnp.where(row == 1, b, jnp.where(row == 2, d, 0.0))).astype(BF16)

    def judge_piece(i):
        m, j = i // PIECES, i % PIECES
        piece(i).wait()
        lifted = jnp.dot(S.FT[...], S.TP[i % SLOTS], preferred_element_type=F32)
        lifted = jnp.sum(lifted, axis=0, keepdims=True)
        if j < 8:
            S.JM[m, j // 4, j % 4] = lifted + mod[m + 1, j // 4 : j // 4 + 1, (j % 4) * COLS : (j % 4 + 1) * COLS]
        else:
            gate = mod[m + 1, 2:3, pl.ds(pl.multiple_of(cb * COLS, COLS), COLS)]
            S.PK[m + 4 : m + 5, :] = lifted + gate
        if i + SLOTS < 2 * PIECES:
            piece(i + SLOTS).start()

    def factors():
        arrived(SC, S.sc_s.at[0], S.sc_r.at[0])
        row = lax.broadcasted_iota(jnp.int32, (8, COLS), 0)
        for m in range(3):
            group = jnp.where(h == 0, sgroup[0:1, m : m + 1], sgroup[1:2, m : m + 1])
            picked = jnp.sum(jnp.where(row == group, SC[m], 0.0), axis=0, keepdims=True)
            if m == 0:
                gate = mod[0, 2:3, pl.ds(pl.multiple_of(cb * COLS, COLS), COLS)]
            else:
                gate = S.PK[m + 3 : m + 4, :]
            S.PK[m : m + 1, :] = gate * picked

    def level():
        return jnp.full((1, COLS), dstep[h], jnp.int32).astype(F32) / 1000.0

    def product(lhs, m, k, first=False):
        ACC = S.ACC
        part = jnp.dot(lhs[k], S.W[m, k].reshape(COLS, COLS), preferred_element_type=F32)
        if first:
            ACC[...] = part
        else:
            ACC[...] += part

    TILE = 64

    def clean_rows(block):
        lev = level()
        here = pl.ds(pl.multiple_of(cb * COLS, COLS), COLS)

        def rows(r, carry):
            at = pl.ds(pl.multiple_of(block * ROWS + r * TILE, TILE), TILE)
            inner = pl.ds(pl.multiple_of(r * TILE, TILE), TILE)
            branch = (S.ACC[at, :] * S.PK[0:1, :]).astype(BF16)
            clean = XG[block, inner, here].astype(F32) + branch.astype(F32)
            noisy = (1.0 - lev) * clean + lev * NS[block, inner, :].astype(F32)
            S.CL[at, :] = clean
            S.NF[at, :] = noisy
            S.SB[at, :] = clean.astype(BF16)
            S.NG[cb, at, :] = noisy.astype(BF16)
            return carry

        lax.fori_loop(0, ROWS // TILE, rows, 0)

    def block_rows(block):
        return pl.ds(block * ROWS, ROWS)

    def noisy_send(block):
        own = S.NG.at[cb, block_rows(block)]
        send(own, own, S.ng_s.at[block, 0], S.ng_r.at[block, 0], dev(h, c, y, z, ol))
        send(own, own, S.ng_s.at[block, 1], S.ng_r.at[block, 1], dev(h, oc, y, z, l))

    far = 2 * ((h + ol) % 2) + c

    def noisy_forward(block):
        got = S.NG.at[far, block_rows(block)]
        arrived(got, S.ng_s.at[block, 0], S.ng_r.at[block, 0])
        send(got, got, S.ng_s.at[block, 2], S.ng_r.at[block, 2], dev(h, oc, y, z, l))

    def noisy_wait(block):
        near = 2 * ((h + l) % 2) + oc
        last = 2 * ((h + ol) % 2) + oc
        arrived(S.NG.at[near, block_rows(block)], S.ng_s.at[block, 1], S.ng_r.at[block, 1])
        arrived(S.NG.at[last, block_rows(block)], S.ng_s.at[block, 2], S.ng_r.at[block, 2])

    def judge_hats(part):
        NG, JH, JM = S.NG, S.JH, S.JM

        def rows(r, carry):
            at = pl.ds(pl.multiple_of(part * 64 + r * 16, 16), 16)
            v = [NG[k, at, :].astype(F32) for k in range(4)]
            total = sum(jnp.sum(t * t, axis=1, keepdims=True) for t in v)
            inv = lax.rsqrt(total / D + RMS_EPS)
            for k in range(4):
                normed = (v[k] * inv).astype(BF16).astype(F32)
                for j in range(2):
                    JH[j, k, at, :] = (normed * (1.0 + JM[j, 1, k]) + JM[j, 0, k]).astype(BF16)
            return carry

        lax.fori_loop(0, 4, rows, 0)

    def return_rows(buf, out, ss, rs):
        here = pl.ds(pl.multiple_of(cb * COLS, COLS), COLS)
        for i, (c_, l_) in enumerate(others):
            block = pl.ds(pl.multiple_of((2 * l_ + c_) * ROWS, ROWS), ROWS)
            send(buf.at[block], out.at[:, here], ss.at[i], rs.at[i], dev(h, c_, y, z, l_))
        block = pl.ds(pl.multiple_of(q * ROWS, ROWS), ROWS)
        own = pltpu.make_async_copy(buf.at[block], out.at[:, here], ss.at[3])
        own.start()
        return own

    def return_wait(out, ss, rs):
        for i, (c_, l_) in enumerate(others):
            arrived(out.at[:, columns(c_, l_)], ss.at[i], rs.at[i])

    def real_rows():
        def rows(r, carry):
            at = pl.ds(pl.multiple_of(r * TILE, TILE), TILE)
            S.RP[at, :] = (S.ACC[at, :] * S.PK[1:2, :]).astype(BF16)
            return carry

        lax.fori_loop(0, GROUP // TILE, rows, 0)

    def spread_rows():
        lev = level()

        def rows(r, total):
            at = pl.ds(pl.multiple_of(r * TILE, TILE), TILE)
            noisy = S.NF[at, :]
            gone = jnp.abs(S.CL[at, :] - (noisy - lev * (noisy + S.RP[at, :].astype(F32))))
            return total + jnp.sum(gone.reshape(TILE // 8, 8, COLS), axis=0)

        total = lax.fori_loop(0, GROUP // TILE, rows, jnp.zeros((8, COLS), F32))
        total = jnp.sum(jnp.sum(total, axis=1, keepdims=True), axis=0, keepdims=True)
        S.SP[...] = jnp.broadcast_to(total, (8, 128))

    def gap_rows():
        lev = level()

        def rows(r, carry):
            at = pl.ds(pl.multiple_of(r * TILE, TILE), TILE)
            fake = (S.ACC[at, :] * S.PK[2:3, :]).astype(BF16).astype(F32)
            gap = lev * (S.RP[at, :].astype(F32) - fake)
            S.GP[at, :] = gap
            S.CT[at, :] = (gap * S.PK[0:1, :]).astype(BF16)
            return carry

        lax.fori_loop(0, GROUP // TILE, rows, 0)

    def spread_group_start():
        S.SPG[q] = S.SP[...]
        for i, (c_, l_) in enumerate(others):
            send(S.SP, S.SPG.at[q], S.sg_s.at[i], S.sg_r.at[i], dev(h, c_, y, z, l_))

    def spread_z_start():
        for i, (c_, l_) in enumerate(others):
            arrived(S.SPG.at[2 * l_ + c_], S.sg_s.at[i], S.sg_r.at[i])
        SPG, SPZ = S.SPG, S.SPZ
        SPZ[z] = (SPG[0] + SPG[1]) + (SPG[2] + SPG[3])
        for j in range(1, NZ):
            send(SPZ.at[z], SPZ.at[z], S.sz_s.at[j], S.sz_r.at[j], dev(h, c, y, zz(j), l))

    def spread_y_start():
        SPZ, SPY = S.SPZ, S.SPY
        for j in range(1, NZ):
            arrived(SPZ.at[zz(-j)], S.sz_s.at[j], S.sz_r.at[j])
        total = SPZ[0]
        for j in range(1, NZ):
            total = total + SPZ[j]
        SPY[y] = total
        for j in range(1, NY):
            send(SPY.at[y], SPY.at[y], S.sy_s.at[j], S.sy_r.at[j], dev(h, c, yy(j), z, l))

    def spread_value():
        SPY = S.SPY
        for j in range(1, NY):
            arrived(SPY.at[yy(-j)], S.sy_s.at[j], S.sy_r.at[j])
        total = SPY[0]
        for j in range(1, NY):
            total = total + SPY[j]
        S.SV[...] = total / CLIP_ELEMENTS + SPREAD_EPS

    def dmd_rows():
        def rows(r, carry):
            at = pl.ds(pl.multiple_of(r * TILE, TILE), TILE)
            S.DB[at, :] = (S.GP[at, :] / S.SV[0:1, 0:1]).astype(BF16)
            return carry

        lax.fori_loop(0, GROUP // TILE, rows, 0)

    G = S.G

    def grad(k, lanes, width):
        block = lax.dot_general(S.H[k], S.CT[:, lanes], (((0,), (0,)), ((), ())), preferred_element_type=F32)
        G[k, :, :, lanes] = block.reshape(NZ, BLK, width)

    def grad_b(k):
        grad(k, LB, CB)

    def grad_a(k):
        grad(k, LA, CA)

    def big_y0(r):
        S.Y0S[r] = G[yy(2), zz(r), :, LB].astype(BF16)
        target = dev(h, c, yy(1 - 2 * way_of[r]), z, l)
        remote(S.Y0S.at[r], S.Y0R.at[r], S.rs_s.at[0], S.b0_r.at[r], target).start()

    def big_y1(r):
        for way in range(2):
            s = 1 - 2 * way
            v = G[yy(s), zz(r), :, LB]
            if way == way_of[r]:
                arrived(S.Y0R.at[r], S.rs_s.at[0], S.b0_r.at[r])
                v = v + S.Y0R[r].astype(F32)
            S.Y1S[r, way] = v.astype(BF16)
            remote(S.Y1S.at[r, way], S.Y1R.at[r, way], S.rs_s.at[1], S.b1_r.at[r], dev(h, c, yy(s), z, l)).start()

    def big_y2(r):
        Y1R = S.Y1R
        arrived(Y1R.at[r], S.rs_s.at[1], S.b1_r.at[r])
        G[y, zz(r), :, LB] = G[y, zz(r), :, LB] + Y1R[r, 0].astype(F32) + Y1R[r, 1].astype(F32)

    def slot(k, way):
        return 0 if k == 1 else 2 * k - 3 + way

    def pair(k):
        return pl.ds(slot(k, 0), 1 if k == 1 else 2)

    def big_z(k, j):
        ZS, ZR = S.ZS, S.ZR
        at = yy(Y_ORDER[j])
        if k > 1:
            arrived(ZR.at[pair(k - 1), j], S.rs_s.at[2], S.a_r.at[k - 2, j])
        for way in range(2):
            s = 1 - 2 * way
            if k == 5 or (k == 1 and way != j % 2):
                continue
            v = G[at, zz(s * (5 - k)), :, LA]
            if k > 2 or (k == 2 and way == j % 2):
                v = v + ZR[slot(k - 1, way), j].astype(F32)
            n = slot(k, way)
            ZS[n, j] = v.astype(BF16)
            remote(ZS.at[n, j], ZR.at[n, j], S.rs_s.at[2], S.a_r.at[k - 1, j], dev(h, c, y, zz(s), l)).start()
        if k == 5:
            G[at, z, :, LA] = G[at, z, :, LA] + ZR[5, j].astype(F32) + ZR[6, j].astype(F32)

    def small_y(step):
        ys, yr = S.ys, S.yr
        halves = (pl.ds(0, CA // 2), pl.ds(CA // 2, CA // 2))
        if step > 0:
            arrived(yr.at[0] if step == 1 else yr.at[1:3], S.rs_s.at[3], S.y_r.at[step - 1])
        for way in range(2):
            s = 1 - 2 * way
            part = halves[way]
            target = dev(h, c, yy(s), z, l)
            if step == 0:
                ys[0, :, part] = G[yy(2), z, :, part].astype(BF16)
                remote(ys.at[0, :, part], yr.at[0, :, part], S.rs_s.at[3], S.y_r.at[0], target).start()
            elif step == 1:
                other = halves[1 - way]
                ys[1 + way, :, part] = (G[yy(s), z, :, part] + yr[0, :, part].astype(F32)).astype(BF16)
                ys[1 + way, :, other] = G[yy(s), z, :, other].astype(BF16)
                remote(ys.at[1 + way], yr.at[1 + way], S.rs_s.at[3], S.y_r.at[1], target).start()
        if step == 2:
            G[y, z, :, LA] = G[y, z, :, LA] + yr[1].astype(F32) + yr[2].astype(F32)

    def small_z(k):
        zs, zr = S.zs, S.zr
        if k > 1:
            arrived(zr.at[0] if k == 2 else zr.at[pair(k - 1)], S.rs_s.at[4], S.z_r.at[k - 2])
        for way in range(2):
            s = 1 - 2 * way
            some = (pl.ds(0, CUT), pl.ds(CUT, BLK - CUT))[way]
            target = dev(h, c, y, zz(s), l)
            n = slot(k, way)
            if k == 1:
                zs[0, some, :] = G[y, zz(4), some, LB].astype(BF16)
                remote(zs.at[0, some], zr.at[0, some], S.rs_s.at[4], S.z_r.at[0], target).start()
            elif k < 5:
                at = zz(s * (5 - k))
                if k > 2:
                    zs[n] = (G[y, at, :, LB] + zr[slot(k - 1, way)].astype(F32)).astype(BF16)
                else:
                    other = (pl.ds(CUT, BLK - CUT), pl.ds(0, CUT))[way]
                    zs[n, some, :] = (G[y, at, some, LB] + zr[0, some, :].astype(F32)).astype(BF16)
                    zs[n, other, :] = G[y, at, other, LB].astype(BF16)
                remote(zs.at[n], zr.at[n], S.rs_s.at[4], S.z_r.at[k - 1], target).start()
        if k == 5:
            G[y, z, :, LB] = G[y, z, :, LB] + zr[5].astype(F32) + zr[6].astype(F32)

    def rings_sent():
        wholes = (S.Y0S, S.Y1S, S.ZS.at[0:7], S.ys.at[0:3], S.zs.at[0:7])
        for i, whole in enumerate(wholes):
            remote(whole, whole, S.rs_s.at[i], S.b0_r.at[0], dev(h, oc, y, z, l)).wait_send()

    tok_own.start()
    noise_own.start()
    for i in range(SLOTS):
        piece(i).start()
    x_prepare()
    features()
    pl.semaphore_wait(barrier, len(greeted))
    x_start(0)
    x_start(1)
    x_start(2)
    tok_near()
    scale_start()
    tok_own.wait()
    gen_hat(q, 0)
    gen_hat(q, 1)
    gen_hat(q, 2)
    gen_hat(q, 3)
    judge_piece(0)
    judge_piece(1)
    judge_piece(2)
    judge_piece(3)
    judge_piece(4)
    judge_piece(5)
    judge_piece(6)
    judge_piece(7)
    judge_piece(8)
    judge_piece(9)
    judge_piece(10)
    judge_piece(11)
    judge_piece(12)
    assemble(0)
    ag_go(0, AY, 1)
    ag_go(0, BZ, 1)
    ag_go(0, FY, 1, 0)
    judge_piece(13)
    arrived(XG.at[q_near], S.tk_s.at[1], S.tk_r.at[1])
    gen_hat(q_near, 0)
    gen_hat(q_near, 1)
    gen_hat(q_near, 2)
    gen_hat(q_near, 3)
    judge_piece(14)
    judge_piece(15)
    judge_piece(16)
    judge_piece(17)
    assemble(1)
    ag_go(1, AY, 1)
    ag_go(1, BZ, 1)
    ag_got(0, AY, 1)
    ag_go(0, AY, 2)
    ag_got(0, BZ, 1)
    ag_go(0, BZ, 2)
    ag_go(0, FY, 1, 1)
    ag_go(0, FY, 1, 7)
    tok_far()
    ag_got(0, FY, 1, 0)
    ag_go(0, FY, 2, 0)
    assemble(2)
    ag_go(2, BZ, 1)
    factors()
    ag_got(0, AY, 2)
    ag_go(0, AZ, 1, 0)
    ag_got(0, FY, 1, 1)
    ag_go(0, FY, 2, 1)
    ag_got(0, BZ, 2)
    ag_go(0, BZ, 3)
    ag_go(0, FY, 1, 2)
    ag_go(0, FY, 1, 6)
    ag_go(0, AZ, 1, 1)
    ag_got(0, FY, 1, 7)
    ag_go(0, FY, 2, 7)
    ag_got(0, AZ, 1, 0)
    ag_go(0, AZ, 2, 0)
    ag_got(0, FY, 1, 2)
    ag_go(0, FY, 2, 2)
    ag_got(1, AY, 1)
    ag_go(1, AY, 2)
    ag_got(0, BZ, 3)
    ag_go(0, BZ, 4)
    ag_go(0, FY, 1, 3)
    ag_go(0, FY, 1, 5)
    ag_got(1, BZ, 1)
    ag_go(1, BZ, 2)
    ag_got(0, FY, 1, 6)
    ag_go(0, FY, 2, 6)
    ag_got(0, AZ, 1, 1)
    ag_go(0, AZ, 2, 1)
    ag_go(2, AY, 1)
    ag_got(0, FY, 1, 3)
    ag_go(0, FY, 2, 3)
    ag_got(0, AZ, 2, 0)
    ag_go(0, AZ, 3, 0)
    ag_got(0, BZ, 4)
    ag_go(0, FY, 1, 4)
    ag_got(0, FY, 1, 5)
    ag_go(0, FY, 2, 5)
    ag_got(1, BZ, 2)
    ag_go(1, BZ, 3)
    ag_got(2, AY, 1)
    ag_go(2, AY, 2)
    ag_got(0, AZ, 2, 1)
    ag_go(0, AZ, 3, 1)
    ag_got(0, FY, 1, 4)
    ag_go(0, FY, 2, 4)
    ag_got(0, AZ, 3, 0)
    ag_go(0, AZ, 4, 0)
    tok_forward()
    noise_send(0)
    noise_send(1)
    noise_send(2)
    gen_hat(q_far, 0)
    gen_hat(q_far, 1)
    gen_hat(q_far, 2)
    gen_hat(q_far, 3)
    ag_got(1, BZ, 3)
    ag_go(1, BZ, 4)
    ag_got(0, AZ, 3, 1)
    ag_go(0, AZ, 4, 1)
    ag_got(1, AY, 2)
    ag_go(1, AZ, 1, 0)
    arrived(XG.at[q_last], S.tk_s.at[2], S.tk_r.at[2])
    gen_hat(q_last, 0)
    gen_hat(q_last, 1)
    ag_got(1, BZ, 4)
    ag_go(1, BY, 1, 0)
    ag_go(1, AZ, 1, 1)
    gen_hat(q_last, 2)
    gen_hat(q_last, 3)
    ag_got(0, AZ, 4, 0)
    ag_got(0, AZ, 4, 1)
    product(S.H, 0, y, True)
    ag_got(2, BZ, 1)
    ag_go(2, BZ, 2)
    product(S.H, 0, yy(1))
    product(S.H, 0, yy(-1))
    ag_got(1, AZ, 1, 0)
    ag_go(1, AZ, 2, 0)
    ag_got(0, FY, 2, 0)
    ag_got(0, FY, 2, 1)
    ag_got(0, FY, 2, 7)
    ag_got(0, FY, 2, 2)
    ag_got(0, FY, 2, 6)
    ag_got(0, FY, 2, 3)
    ag_got(0, FY, 2, 5)
    ag_got(0, FY, 2, 4)
    product(S.H, 0, yy(2))
    ag_go(1, BY, 1, 1)
    noise_wait()
    clean_rows(0)
    noisy_send(0)
    clean_rows(1)
    noisy_send(1)
    clean_rows(2)
    noisy_send(2)
    ag_got(1, AZ, 1, 1)
    ag_go(1, AZ, 2, 1)
    clean_rows(3)
    noisy_send(3)
    ag_got(2, BZ, 2)
    ag_go(2, BZ, 3)
    ag_got(1, AZ, 2, 0)
    ag_go(1, AZ, 3, 0)
    noisy_forward(0)
    ag_got(1, BY, 1, 0)
    ag_go(1, BY, 2, 0)
    ag_got(1, AZ, 2, 1)
    ag_go(1, AZ, 3, 1)
    ag_got(2, BZ, 3)
    ag_go(2, BZ, 4)
    noisy_wait(0)
    judge_hats(0)
    ag_got(1, BY, 1, 1)
    ag_go(1, BY, 2, 1)
    ag_got(2, AY, 2)
    ag_go(2, AZ, 1, 0)
    judge_hats(1)
    noisy_forward(1)
    ag_got(1, AZ, 3, 0)
    ag_go(1, AZ, 4, 0)
    ag_got(1, AZ, 3, 1)
    ag_go(1, AZ, 4, 1)
    ag_got(2, BZ, 4)
    ag_go(2, BY, 1, 0)
    noisy_wait(1)
    judge_hats(2)
    ag_go(2, AZ, 1, 1)
    judge_hats(3)
    noisy_forward(2)
    ag_got(2, AZ, 1, 0)
    ag_go(2, AZ, 2, 0)
    noisy_wait(2)
    judge_hats(4)
    judge_hats(5)
    noisy_forward(3)
    ag_go(2, BY, 1, 1)
    ag_got(2, AZ, 1, 1)
    ag_go(2, AZ, 2, 1)
    ag_got(2, AZ, 2, 0)
    ag_go(2, AZ, 3, 0)
    noisy_wait(3)
    judge_hats(6)
    judge_hats(7)
    ag_got(1, AZ, 4, 0)
    ag_got(1, AZ, 4, 1)
    product(S.JH.at[0], 1, y, True)
    ag_got(2, AZ, 2, 1)
    ag_go(2, AZ, 3, 1)
    product(S.JH.at[0], 1, yy(1))
    product(S.JH.at[0], 1, yy(-1))
    ag_got(2, BY, 1, 0)
    ag_go(2, BY, 2, 0)
    ag_got(2, AZ, 3, 0)
    ag_go(2, AZ, 4, 0)
    ag_got(1, BY, 2, 0)
    ag_got(1, BY, 2, 1)
    product(S.JH.at[0], 1, yy(2))
    real_rows()
    spread_rows()
    spread_group_start()
    ag_got(2, AZ, 3, 1)
    ag_go(2, AZ, 4, 1)
    ag_got(2, BY, 1, 1)
    ag_go(2, BY, 2, 1)
    sample_own = return_rows(S.SB, out_s, S.sm_s, S.sm_r)
    ag_got(2, AZ, 4, 0)
    ag_got(2, AZ, 4, 1)
    product(S.JH.at[1], 2, y, True)
    product(S.JH.at[1], 2, yy(1))
    product(S.JH.at[1], 2, yy(-1))
    ag_got(2, BY, 2, 0)
    ag_got(2, BY, 2, 1)
    product(S.JH.at[1], 2, yy(2))
    gap_rows()
    spread_z_start()
    grad_b(yy(2))
    big_y0(4)
    big_y0(3)
    grad_a(yy(2))
    big_y0(5)
    big_z(1, 0)
    grad_a(yy(1))
    big_y0(2)
    big_z(1, 1)
    grad_a(yy(-1))
    big_y0(6)
    big_z(1, 2)
    grad_a(yy(0))
    big_y0(1)
    big_z(1, 3)
    grad_b(yy(1))
    big_z(2, 0)
    grad_b(yy(-1))
    big_y0(7)
    big_z(2, 1)
    grad_b(y)
    big_y0(0)
    big_z(2, 2)
    spread_y_start()
    big_y1(4)
    big_z(2, 3)
    ag_sent(0)
    ag_sent(1)
    ag_sent(2)
    big_z(3, 0)
    big_y1(3)
    big_z(3, 1)
    spread_value()
    dmd_rows()
    big_y1(5)
    big_z(3, 2)
    dmd_own = return_rows(S.DB, out_d, S.dm_s, S.dm_r)
    big_z(3, 3)
    big_y2(4)
    small_z(1)
    big_y1(2)
    big_z(4, 0)
    big_y2(3)
    big_y1(6)
    big_z(4, 1)
    big_y2(5)
    big_y1(1)
    big_z(4, 2)
    small_z(2)
    big_y2(2)
    big_y1(7)
    big_z(5, 0)
    small_y(0)
    drain()
    big_z(4, 3)
    big_y2(6)
    big_z(5, 1)
    big_y1(0)
    big_z(5, 2)
    big_y2(1)
    small_z(3)
    big_y2(7)
    small_y(1)
    big_z(5, 3)
    big_y2(0)
    small_z(4)
    small_y(2)
    small_z(5)
    GF, OW = S.GF, S.OW
    done = G[y, z] / S.SV[0:1, 0:1] / TOKENS

    def own_row(row, slot, target):
        return remote(GF.at[row], OW.at[slot], S.ow_s.at[row], S.ow_r.at[slot], target)

    for row in range(2):
        GF[row] = done[row * HALF : (row + 1) * HALF]

    @pl.when(l == 0)
    def _():
        OW[0] = GF[0]
        own_row(1, 0, dev(h, c, y, z, 1)).start()

    @pl.when(l == 1)
    def _():
        own_row(0, 1, dev(oh, c, y, z, 0)).start()
        own_row(1, 1, dev(oh, c, y, z, 1)).start()
        arrived(OW.at[0], S.ow_s.at[0], S.ow_r.at[0])

    arrived(OW.at[1], S.ow_s.at[1], S.ow_r.at[1])
    out_w[...] = OW[0] + OW[1]
    return_wait(out_s, S.sm_s, S.sm_r)
    return_wait(out_d, S.dm_s, S.dm_r)
    sample_own.wait()
    dmd_own.wait()
    rings_sent()
    drain()
    for m in range(3):
        x_first(m, 0).wait_send()

    @pl.when(l == 0)
    def _():
        scale_copy().wait_send()
        own_row(1, 0, dev(h, c, y, z, 1)).wait_send()

    @pl.when(l == 1)
    def _():
        for m in range(3):
            x_second(m).wait_send()
        own_row(0, 1, dev(oh, c, y, z, 0)).wait_send()
        own_row(1, 1, dev(oh, c, y, z, 1)).wait_send()


def copy_results(a_in, b_in, c_in, a_out, b_out, c_out):
    a_out[...] = a_in[...]
    b_out[...] = b_in[...]
    c_out[...] = c_in[...]


def on_device(gi, noise, dmd_step, scale_group, wg, wt, wc, scales, mod, tproj):
    vmem = pl.BlockSpec(memory_space=pltpu.VMEM)
    smem = pl.BlockSpec(memory_space=pltpu.SMEM)
    hbm = pl.BlockSpec(memory_space=pl.ANY)
    out_shape = (
        jax.ShapeDtypeStruct((ROWS, D), BF16),
        jax.ShapeDtypeStruct((ROWS, D), BF16),
        jax.ShapeDtypeStruct((HALF, COLS), F32),
    )
    results = pl.pallas_call(
        kernel,
        out_shape=out_shape,
        in_specs=[hbm, hbm, smem, vmem, vmem, vmem, vmem, hbm, vmem, hbm],
        out_specs=(hbm, hbm, vmem),
        scratch_shapes=list(scratch_table().values()),
        compiler_params=pltpu.CompilerParams(
            collective_id=0, has_side_effects=True, vmem_limit_bytes=64 * 1024 * 1024 - 65536
        ),
    )(gi, noise, dmd_step, scale_group.T, wg, wt, wc, scales, mod, tproj)
    half = pl.BlockSpec((ROWS // 2, D), lambda i: (i, 0))
    whole = pl.BlockSpec((HALF, COLS), lambda i: (0, 0))
    return pl.pallas_call(
        copy_results,
        grid=(2,),
        out_shape=out_shape,
        in_specs=[half, half, whole],
        out_specs=(half, half, whole),
    )(*results)


def solution(mesh):
    return jax.shard_map(
        on_device,
        mesh=mesh,
        in_specs=(
            P(("dp", "fsdp"), None),
            P(("dp", "fsdp"), None),
            P(),
            P(),
            P("fsdp", "dp"),
            P("fsdp", "dp"),
            P("fsdp", "dp"),
            P(None, None, "dp"),
            P(),
            P(),
        ),
        out_specs=(P(("dp", "fsdp"), None), P(("dp", "fsdp"), None), P("fsdp", "dp")),
        check_vma=False,
    )
```

time: 1490 us -> 122 us (0.08); the launches traced: 1470 us -> 120 us
  waiting for transfers between devices: 1230 us -> 0 us
  blocking collectives: 120 us -> 0 us
  Pallas kernels: 0 us -> 119 us
  local copies, waits for them, and re-layouts: 37.1 us -> 0 us
  other arithmetic: 28.2 us -> 0 us
  matrix products: 27.3 us -> 0 us
    all_gather x5 -> x0, waiting for transfers between devices: 932 us -> none  [the longest x1 290 us: on_device(): lax.all_gather(critic_codes, 'fsdp', axis=0, tiled=True)]
    unnamed x7 -> x0, waiting for transfers between devices: 292 us -> none
    pallas_call x0 -> x2, Pallas kernels: none -> 119 us  [the longest x1 117 us: on_device(): pl.pallas_call(kernel, out_shape=out_shape, in_specs=[hbm, hbm, smem, vme...]
    psum x1 -> x0, blocking collectives: 96.6 us -> none  [on_device(): totals = lax.psum(clip_pick * partial_value, ('dp', 'fsdp'))]
    dot_general x6 -> x0, matrix products: 27.3 us -> none  [the longest x1 6.69 us: on_device(): lax.dot_general(hat_group, cotangent, (((0,), (0,)), ((), ())), preferred...]
    all_to_all x1 -> x0, blocking collectives: 23 us -> none  [return_tokens(): lax.all_to_all(stacked, 'dp', split_axis=1, concat_axis=2, tiled=True)]
  transfers between devices with their start and end apart: 7 -> 0, of which waited for: 7 -> 0; matrix products, arithmetic and copies ran while one was open for 3% -> 0% of each run, Pallas kernels for 0% -> 0%
where the time goes in v2:
time: 122 us; the launch traced here: 120 us
  Pallas kernels  119 us (98%)
    pallas_call x1, Pallas kernels, on_device(): pl.pallas_call(kernel, out_shape=out_shape, in_specs=[hbm, hbm, smem, vme...  117 us

profile of v2, /device:TPU:8, one launch (start us, length us, event | category | flops | bytes accessed | tf_op | source)
XLA Modules:
  0.0 120.2 jit_solution(13388536255510483087)
XLA Ops:
  0.6 117.2 %shard_map.121 = (bf16[128,2560]{1,0:T(8,128)(2,1)}, bf16[128,2560]{1,0:T(8,128)(2,1)}, f32[40,640]{1,0:T(8,128)}) custom-call(bf16[128,2560]{1,0:T(8,128)(2,1)} %gi.1, bf16[128,2560]{1,0:T(8,128)(2,1)} %noise.1, s32[2]{0:T(128)} %dstep.1, s32[2,3]{1,0:T(2,128)} %bitcast.1, bf16[40,640]{1,0:T(8,128)(2,1)} %wg.1, bf16[40,640]{1,0:T(8,128)(2,1)} %wt.1, ...), custom_call_target="tpu_custom_call" | custom-call | tf_op jit(solution)/shard_map/pallas_call | solution.py:989
  117.8 2.2 %shard_map.122 = (bf16[128,2560]{1,0:T(8,128)(2,1)}, bf16[128,2560]{1,0:T(8,128)(2,1)}, f32[40,640]{1,0:T(8,128)}) custom-call(bf16[128,2560]{1,0:T(8,128)(2,1)} %get-tuple-element.6.a_in, bf16[128,2560]{1,0:T(8,128)(2,1)} %get-tuple-element.7.b_in, f32[40,640]{1,0:T(8,128)} %get-tuple-element.8.c_in), custom_call_target="tpu_custom_call" | custom-call | tf_op jit(solution)/shard_map/pallas_call | solution.py:1001

commit v3 on v2

--- a/solution.py
+++ b/solution.py
@@ -31,7 +31,25 @@
 TPC = 640
 PIECES = 9
 SLOTS = 4
-AY, AZ, BZ, BY, FY = range(5)
+AY, AZ, BZ, BY, FY, FZ, XY, XZ = range(8)
+FINE_Y, FINE_Z = (0, 1, 2), (0, 1, 2)
+SHARED = (1, 2)
+
+
+def ag_table():
+    steps = []
+    for m in range(3):
+        steps += [(m, AY, k, 0) for k in (1, 2)] + [(m, BZ, k, 0) for k in (1, 2, 3, 4)]
+        if m in SHARED:
+            steps += [(m, FZ, k, i) for k in (1, 2, 3, 4) for i in range(3)] + [(m, XZ, k, 0) for k in (1, 2, 3, 4)]
+            steps += [(m, FY, k, i) for k in (1, 2) for i in (0, 1, 7, 4, 8, 9)] + [(m, XY, k, i) for k in (1, 2) for i in (8, 9)]
+            continue
+        steps += [(m, FZ, k, i) for k in (1, 2, 3, 4) for i in range(4)] if m in FINE_Z else [(m, AZ, k, i) for k in (1, 2, 3, 4) for i in range(2)]
+        steps += [(m, FY, k, i) for k in (1, 2) for i in range(8)] if m in FINE_Y else [(m, BY, k, i) for k in (1, 2) for i in range(2)]
+    return {step: n for n, step in enumerate(steps)}
+
+
+AG_SEMS = ag_table()
 
 
 def scratch_table():
@@ -74,37 +92,36 @@
         SPG=vmem((4, 8, 128), F32),
         SPZ=vmem((NZ, 8, 128), F32),
         SPY=vmem((NY, 8, 128), F32),
-        GF=vmem((2, HALF, COLS), F32),
-        OW=vmem((2, HALF, COLS), F32),
-        ag_s=dma((3, 4)),
-        ag_r=dma((3, 18)),
-        fy_r=dma((16,)),
+        GF=vmem((2, PAD, COLS), BF16),
+        OW=vmem((2, PAD, COLS), BF16),
+        ag_s=dma((3, 6)),
+        ag_r=dma((len(AG_SEMS),)),
         x_s=dma((3, 2)),
         x_r=dma((3, 2)),
-        tk_s=dma((4,)),
-        tk_r=dma((4,)),
-        ns_s=dma((4,)),
-        ns_r=dma((4,)),
-        ng_s=dma((4, 3)),
-        ng_r=dma((4, 3)),
-        sm_s=dma((4,)),
-        sm_r=dma((4,)),
-        dm_s=dma((4,)),
-        dm_r=dma((4,)),
+        tk_s=dma((2,)),
+        tk_r=dma((3,)),
+        ns_s=dma((2,)),
+        ns_r=dma((1,)),
+        ng_s=dma((1,)),
+        ng_r=dma((4, 2)),
+        sm_s=dma((2,)),
+        sm_r=dma((1,)),
+        dm_s=dma((2,)),
+        dm_r=dma((1,)),
         sc_s=dma((1,)),
         sc_r=dma((1,)),
         tp_m=dma((SLOTS,)),
-        sg_s=dma((4,)),
-        sg_r=dma((4,)),
-        sz_s=dma((NZ,)),
-        sz_r=dma((NZ,)),
-        sy_s=dma((NY,)),
-        sy_r=dma((NY,)),
+        sg_s=dma((1,)),
+        sg_r=dma((1,)),
+        sz_s=dma((1,)),
+        sz_r=dma((1,)),
+        sy_s=dma((1,)),
+        sy_r=dma((1,)),
         rs_s=dma((5,)),
         b0_r=dma((NZ,)),
         b1_r=dma((NZ,)),
         a_r=dma((4, NY)),
-        y_r=dma((2,)),
+        y_r=dma((1,)),
         z_r=dma((4,)),
         ow_s=dma((2,)),
         ow_r=dma((2,)),
@@ -133,22 +150,27 @@
     def zz(step):
         return (z + step + NZ) % NZ
 
-    started = []
-
     def remote(src, dst, ss, rs, target):
         return pltpu.make_async_remote_copy(
             src_ref=src, dst_ref=dst, send_sem=ss, recv_sem=rs, device_id=target, device_id_type=MESH_ID
         )
 
     def send(src, dst, ss, rs, target):
-        copy = remote(src, dst, ss, rs, target)
-        copy.start()
-        started.append(copy)
+        remote(src, dst, ss, rs, target).start()
 
     def drain():
-        for copy in started:
-            copy.wait_send()
-        started.clear()
+        wholes = (
+            (XG.at[0:3], S.tk_s),
+            (NS.at[0:3], S.ns_s),
+            (S.NG.at[0:3], S.ng_s),
+            (NS.at[0:3], S.sm_s),
+            (NS.at[0:3], S.dm_s),
+            (S.SPG.at[0:3], S.sg_s),
+            (S.SPZ.at[0:7], S.sz_s),
+            (S.SPY.at[0:3], S.sy_s),
+        )
+        for whole, ss in wholes:
+            remote(whole, whole, ss.at[0], S.rs_s.at[0], dev(h, oc, y, z, l)).wait_send()
 
     def arrived(dst, ss, rs):
         remote(dst, dst, ss, rs, dev(h, oc, y, z, l)).wait_recv()
@@ -164,7 +186,16 @@
     LA, LB = pl.ds(0, CA), pl.ds(CA, CB)
     Z_ORDER = (4, 3, 5, 2, 6, 1, 7, 0)
     Y_ORDER = (2, 1, -1, 0)
+    Z_FINE = (0, 1, -1, 2)
     way_of = {r: i % 2 for i, r in enumerate(Z_ORDER)}
+    way_of.update({8: 1, 9: 0})
+
+    def along_z(i, l_):
+        return {8: 2 + 4 * l_, 9: 3 + 2 * l_}.get(i, i)
+
+    def along_y(m, i, l_):
+        return 2 - 3 * l_ if i == 2 and m in SHARED else Z_FINE[i]
+
 
     def ag_copies(m, op, k, i):
         W = S.W
@@ -172,34 +203,47 @@
             s = 1 - 2 * way
             if op == AY:
                 if k == 1:
-                    yield W.at[m, y, z, :, LA], W.at[m, yy(-s), z, :, LA], way
+                    yield W.at[m, y, z, :, LA], W.at[m, yy(-s), z, :, LA], s
                 else:
                     part = pl.ds(way * (CA // 2), CA // 2)
-                    yield W.at[m, yy(-s), z, :, part], W.at[m, yy(2), z, :, part], way
+                    yield W.at[m, yy(-s), z, :, part], W.at[m, yy(2), z, :, part], s
             elif op == AZ:
                 if k < 4 or way == i:
                     some = pl.ds(2 * i, 2)
-                    yield W.at[m, some, zz(-s * (k - 1)), :, LA], W.at[m, some, zz(-s * k), :, LA], way
+                    yield W.at[m, some, zz(-s * (k - 1)), :, LA], W.at[m, some, zz(-s * k), :, LA], s
+            elif op == FZ:
+                if k < 4 or way == i % 2:
+                    at = yy(along_y(m, i, l))
+                    yield W.at[m, at, zz(-s * (k - 1)), :, LA], W.at[m, at, zz(-s * k), :, LA], s
+            elif op == XZ:
+                if k < 4 or way == 0:
+                    mine, theirs = yy(along_y(m, 2, l)), yy(along_y(m, 2, ol))
+                    yield W.at[m, mine, zz(-s * k), :, LA], W.at[m, theirs, zz(-s * k), :, LA], s
+            elif op == XY:
+                if k == 1 or way == 0:
+                    at = yy(-s) if k == 1 else yy(2)
+                    yield W.at[m, at, zz(along_z(i, l)), :, LB], W.at[m, at, zz(along_z(i, ol)), :, LB], s
             elif op == BZ:
                 some = pl.ds(0, BLK) if k < 4 else (pl.ds(0, CUT), pl.ds(CUT, BLK - CUT))[way]
-                yield W.at[m, y, zz(-s * (k - 1)), some, LB], W.at[m, y, zz(-s * k), some, LB], way
+                yield W.at[m, y, zz(-s * (k - 1)), some, LB], W.at[m, y, zz(-s * k), some, LB], s
             else:
-                some = pl.ds(4 * i, 4) if op == BY else zz(i)
+                some = pl.ds(4 * i, 4) if op == BY else zz(along_z(i, l))
                 if k == 1:
-                    yield W.at[m, y, some, :, LB], W.at[m, yy(-s), some, :, LB], way
+                    yield W.at[m, y, some, :, LB], W.at[m, yy(-s), some, :, LB], s
                 elif way == (i if op == BY else way_of[i]):
-                    yield W.at[m, yy(-s), some, :, LB], W.at[m, yy(2), some, :, LB], way
+                    yield W.at[m, yy(-s), some, :, LB], W.at[m, yy(2), some, :, LB], s
 
     def ag_sems(m, op, k, i):
-        n = {AY: k - 1, AZ: 2 + (k - 1) * 2 + i, BZ: 9 + k, BY: 12 + 2 * k + i, FY: 18 + 8 * (k - 1) + i}[op]
-        group = {AY: 0, AZ: 1, BZ: 2, BY: 3, FY: 3}[op]
-        return S.ag_s.at[m, group], S.fy_r.at[n - 18] if op == FY else S.ag_r.at[m, n]
+        group = {AY: 0, AZ: 1, FZ: 1, BZ: 2, BY: 3, FY: 3, XY: 4, XZ: 5}[op]
+        return S.ag_s.at[m, group], S.ag_r.at[AG_SEMS[m, op, k, i]]
 
     def ag_go(m, op, k, i=0):
         ss, rs = ag_sems(m, op, k, i)
-        for src, _, way in ag_copies(m, op, k, i):
-            s = 1 - 2 * way
-            target = dev(h, c, y, zz(s), l) if op in (AZ, BZ) else dev(h, c, yy(s), z, l)
+        for src, _, s in ag_copies(m, op, k, i):
+            if op in (XY, XZ):
+                target = dev(oh, c, y, z, ol)
+            else:
+                target = dev(h, c, y, zz(s), l) if op in (AZ, BZ, FZ) else dev(h, c, yy(s), z, l)
             remote(src, src, ss, rs, target).start()
 
     def ag_got(m, op, k, i=0):
@@ -209,6 +253,8 @@
             both = W.at[m, 0:2, z, :, LA] if k == 1 else W.at[m, 0, z, :, LA]
         elif op == AZ:
             both = W.at[m, :, z, :, LA] if k < 4 else W.at[m, 0:2, z, :, LA]
+        elif op in (FZ, XZ):
+            both = W.at[m, 0:2, z, :, LA] if k < 4 else W.at[m, 0, z, :, LA]
         elif op == BZ:
             both = W.at[m, 0, 0:2, :, LB] if k < 4 else W.at[m, 0, 0, :, LB]
         elif op == BY:
@@ -219,10 +265,12 @@
 
     def ag_sent(m):
         W = S.W
-        for group, whole in enumerate(
-            (W.at[m, 0:3, 0, :, LA], W.at[m, :, 0:7, :, LA], W.at[m, 0, 0:7, :, LB], W.at[m, 0:3, :, :, LB])
-        ):
-            remote(whole, whole, S.ag_s.at[m, group], S.ag_r.at[m, 0], dev(h, oc, y, z, l)).wait_send()
+        wholes = [W.at[m, 0:3, 0, :, LA], W.at[m, :, 0:7, :, LA], W.at[m, 0, 0:7, :, LB], W.at[m, 0:3, :, :, LB]]
+        if m in SHARED:
+            wholes[1], wholes[3] = W.at[m, 0:3, 0:7, :, LA], W.at[m, 0:3, 0:6, :, LB]
+            wholes += [W.at[m, 0, 0:6, :, LB], W.at[m, 0, 0:7, :, LA]]
+        for group, whole in enumerate(wholes):
+            remote(whole, whole, S.ag_s.at[m, group], S.ag_r.at[0], dev(h, oc, y, z, l)).wait_send()
 
     XO, XS = S.XO, S.XS
 
@@ -262,17 +310,17 @@
         S.W[m, y, z] = jnp.concatenate(both, axis=0).astype(BF16)
 
     XG, NS, SC = S.XG, S.NS, S.SC
-    tok_own = pltpu.make_async_copy(gi, XG.at[q], S.tk_s.at[3])
+    tok_own = pltpu.make_async_copy(gi, XG.at[q], S.tk_s.at[1])
 
     def tok_near():
-        send(gi, XG.at[q], S.tk_s.at[1], S.tk_r.at[1], dev(h, oc, y, z, l))
+        send(gi, XG.at[q], S.tk_s.at[0], S.tk_r.at[1], dev(h, oc, y, z, l))
 
     def tok_far():
         send(gi, XG.at[q], S.tk_s.at[0], S.tk_r.at[0], dev(h, c, y, z, ol))
 
     def tok_forward():
         arrived(XG.at[q_far], S.tk_s.at[0], S.tk_r.at[0])
-        send(XG.at[q_far], XG.at[q_far], S.tk_s.at[2], S.tk_r.at[2], dev(h, oc, y, z, l))
+        send(XG.at[q_far], XG.at[q_far], S.tk_s.at[0], S.tk_r.at[2], dev(h, oc, y, z, l))
 
     q_far, q_near, q_last = 2 * ol + c, 2 * l + oc, 2 * ol + oc
 
@@ -283,14 +331,13 @@
 
     def noise_send(i):
         c_, l_ = others[i]
-        send(noise.at[:, columns(c_, l_)], NS.at[q], S.ns_s.at[i], S.ns_r.at[i], dev(h, c_, y, z, l_))
+        send(noise.at[:, columns(c_, l_)], NS.at[q], S.ns_s.at[0], S.ns_r.at[0], dev(h, c_, y, z, l_))
 
     def noise_wait():
         noise_own.wait()
-        for i, (c_, l_) in enumerate(others):
-            arrived(NS.at[2 * l_ + c_], S.ns_s.at[i], S.ns_r.at[i])
-
-    noise_own = pltpu.make_async_copy(noise.at[:, columns(c, l)], NS.at[q], S.ns_s.at[3])
+        arrived(NS.at[0:3], S.ns_s.at[0], S.ns_r.at[0])
+
+    noise_own = pltpu.make_async_copy(noise.at[:, columns(c, l)], NS.at[q], S.ns_s.at[1])
 
     def scale_copy():
         return remote(scales, SC, S.sc_s.at[0], S.sc_r.at[0], dev(oh, c, y, z, 1))
@@ -400,21 +447,18 @@
 
     def noisy_send(block):
         own = S.NG.at[cb, block_rows(block)]
-        send(own, own, S.ng_s.at[block, 0], S.ng_r.at[block, 0], dev(h, c, y, z, ol))
-        send(own, own, S.ng_s.at[block, 1], S.ng_r.at[block, 1], dev(h, oc, y, z, l))
+        send(own, own, S.ng_s.at[0], S.ng_r.at[block, 0], dev(h, c, y, z, ol))
+        send(own, own, S.ng_s.at[0], S.ng_r.at[block, 1], dev(h, oc, y, z, l))
 
     far = 2 * ((h + ol) % 2) + c
 
     def noisy_forward(block):
         got = S.NG.at[far, block_rows(block)]
-        arrived(got, S.ng_s.at[block, 0], S.ng_r.at[block, 0])
-        send(got, got, S.ng_s.at[block, 2], S.ng_r.at[block, 2], dev(h, oc, y, z, l))
+        arrived(got, S.ng_s.at[0], S.ng_r.at[block, 0])
+        send(got, got, S.ng_s.at[0], S.ng_r.at[block, 1], dev(h, oc, y, z, l))
 
     def noisy_wait(block):
-        near = 2 * ((h + l) % 2) + oc
-        last = 2 * ((h + ol) % 2) + oc
-        arrived(S.NG.at[near, block_rows(block)], S.ng_s.at[block, 1], S.ng_r.at[block, 1])
-        arrived(S.NG.at[last, block_rows(block)], S.ng_s.at[block, 2], S.ng_r.at[block, 2])
+        arrived(S.NG.at[0:2, block_rows(block)], S.ng_s.at[0], S.ng_r.at[block, 1])
 
     def judge_hats(part):
         NG, JH, JM = S.NG, S.JH, S.JM
@@ -436,38 +480,46 @@
         here = pl.ds(pl.multiple_of(cb * COLS, COLS), COLS)
         for i, (c_, l_) in enumerate(others):
             block = pl.ds(pl.multiple_of((2 * l_ + c_) * ROWS, ROWS), ROWS)
-            send(buf.at[block], out.at[:, here], ss.at[i], rs.at[i], dev(h, c_, y, z, l_))
+            send(buf.at[block], out.at[:, here], ss.at[0], rs.at[0], dev(h, c_, y, z, l_))
         block = pl.ds(pl.multiple_of(q * ROWS, ROWS), ROWS)
-        own = pltpu.make_async_copy(buf.at[block], out.at[:, here], ss.at[3])
+        own = pltpu.make_async_copy(buf.at[block], out.at[:, here], ss.at[1])
         own.start()
         return own
 
     def return_wait(out, ss, rs):
-        for i, (c_, l_) in enumerate(others):
-            arrived(out.at[:, columns(c_, l_)], ss.at[i], rs.at[i])
-
-    def real_rows():
-        def rows(r, carry):
-            at = pl.ds(pl.multiple_of(r * TILE, TILE), TILE)
-            S.RP[at, :] = (S.ACC[at, :] * S.PK[1:2, :]).astype(BF16)
-            return carry
-
-        lax.fori_loop(0, GROUP // TILE, rows, 0)
-
-    def spread_rows():
+        arrived(NS.at[0:3], ss.at[0], rs.at[0])
+
+    def judged(m, half):
+        ACC = S.ACC
+        at = pl.ds(half * (GROUP // 2), GROUP // 2)
+        for k in range(4):
+            part = jnp.dot(S.JH[m - 1, k, at, :], S.W[m, k].reshape(COLS, COLS), preferred_element_type=F32)
+            if k == 0:
+                ACC[at, :] = part
+            else:
+                ACC[at, :] += part
+
+    def half_tiles(half, body, carry):
+        tiles = GROUP // 2 // TILE
+        return lax.fori_loop(half * tiles, (half + 1) * tiles, body, carry)
+
+    def real_rows(half):
         lev = level()
 
         def rows(r, total):
             at = pl.ds(pl.multiple_of(r * TILE, TILE), TILE)
+            real = (S.ACC[at, :] * S.PK[1:2, :]).astype(BF16)
+            S.RP[at, :] = real
             noisy = S.NF[at, :]
-            gone = jnp.abs(S.CL[at, :] - (noisy - lev * (noisy + S.RP[at, :].astype(F32))))
+            gone = jnp.abs(S.CL[at, :] - (noisy - lev * (noisy + real.astype(F32))))
             return total + jnp.sum(gone.reshape(TILE // 8, 8, COLS), axis=0)
 
-        total = lax.fori_loop(0, GROUP // TILE, rows, jnp.zeros((8, COLS), F32))
+        total = half_tiles(half, rows, jnp.zeros((8, COLS), F32))
         total = jnp.sum(jnp.sum(total, axis=1, keepdims=True), axis=0, keepdims=True)
-        S.SP[...] = jnp.broadcast_to(total, (8, 128))
-
-    def gap_rows():
+        total = jnp.broadcast_to(total, (8, 128))
+        S.SP[...] = total if half == 0 else S.SP[...] + total
+
+    def gap_rows(half):
         lev = level()
 
         def rows(r, carry):
@@ -478,36 +530,33 @@
             S.CT[at, :] = (gap * S.PK[0:1, :]).astype(BF16)
             return carry
 
-        lax.fori_loop(0, GROUP // TILE, rows, 0)
+        half_tiles(half, rows, 0)
 
     def spread_group_start():
         S.SPG[q] = S.SP[...]
-        for i, (c_, l_) in enumerate(others):
-            send(S.SP, S.SPG.at[q], S.sg_s.at[i], S.sg_r.at[i], dev(h, c_, y, z, l_))
+        for c_, l_ in others:
+            send(S.SP, S.SPG.at[q], S.sg_s.at[0], S.sg_r.at[0], dev(h, c_, y, z, l_))
 
     def spread_z_start():
-        for i, (c_, l_) in enumerate(others):
-            arrived(S.SPG.at[2 * l_ + c_], S.sg_s.at[i], S.sg_r.at[i])
         SPG, SPZ = S.SPG, S.SPZ
+        arrived(SPG.at[0:3], S.sg_s.at[0], S.sg_r.at[0])
         SPZ[z] = (SPG[0] + SPG[1]) + (SPG[2] + SPG[3])
         for j in range(1, NZ):
-            send(SPZ.at[z], SPZ.at[z], S.sz_s.at[j], S.sz_r.at[j], dev(h, c, y, zz(j), l))
+            send(SPZ.at[z], SPZ.at[z], S.sz_s.at[0], S.sz_r.at[0], dev(h, c, y, zz(j), l))
 
     def spread_y_start():
         SPZ, SPY = S.SPZ, S.SPY
-        for j in range(1, NZ):
-            arrived(SPZ.at[zz(-j)], S.sz_s.at[j], S.sz_r.at[j])
+        arrived(SPZ.at[0:7], S.sz_s.at[0], S.sz_r.at[0])
         total = SPZ[0]
         for j in range(1, NZ):
             total = total + SPZ[j]
         SPY[y] = total
         for j in range(1, NY):
-            send(SPY.at[y], SPY.at[y], S.sy_s.at[j], S.sy_r.at[j], dev(h, c, yy(j), z, l))
+            send(SPY.at[y], SPY.at[y], S.sy_s.at[0], S.sy_r.at[0], dev(h, c, yy(j), z, l))
 
     def spread_value():
         SPY = S.SPY
-        for j in range(1, NY):
-            arrived(SPY.at[yy(-j)], S.sy_s.at[j], S.sy_r.at[j])
+        arrived(SPY.at[0:3], S.sy_s.at[0], S.sy_r.at[0])
         total = SPY[0]
         for j in range(1, NY):
             total = total + SPY[j]
@@ -577,25 +626,16 @@
         if k == 5:
             G[at, z, :, LA] = G[at, z, :, LA] + ZR[5, j].astype(F32) + ZR[6, j].astype(F32)
 
-    def small_y(step):
+    def small_y(j):
         ys, yr = S.ys, S.yr
-        halves = (pl.ds(0, CA // 2), pl.ds(CA // 2, CA // 2))
-        if step > 0:
-            arrived(yr.at[0] if step == 1 else yr.at[1:3], S.rs_s.at[3], S.y_r.at[step - 1])
-        for way in range(2):
-            s = 1 - 2 * way
-            part = halves[way]
-            target = dev(h, c, yy(s), z, l)
-            if step == 0:
-                ys[0, :, part] = G[yy(2), z, :, part].astype(BF16)
-                remote(ys.at[0, :, part], yr.at[0, :, part], S.rs_s.at[3], S.y_r.at[0], target).start()
-            elif step == 1:
-                other = halves[1 - way]
-                ys[1 + way, :, part] = (G[yy(s), z, :, part] + yr[0, :, part].astype(F32)).astype(BF16)
-                ys[1 + way, :, other] = G[yy(s), z, :, other].astype(BF16)
-                remote(ys.at[1 + way], yr.at[1 + way], S.rs_s.at[3], S.y_r.at[1], target).start()
-        if step == 2:
-            G[y, z, :, LA] = G[y, z, :, LA] + yr[1].astype(F32) + yr[2].astype(F32)
+        if j < 3:
+            at = yy(Y_ORDER[j])
+            ys[j] = G[at, z, :, LA].astype(BF16)
+            remote(ys.at[j], yr.at[j], S.rs_s.at[3], S.y_r.at[0], dev(h, c, at, z, l)).start()
+        else:
+            arrived(yr.at[0:3], S.rs_s.at[3], S.y_r.at[0])
+            total = yr[0].astype(F32) + yr[1].astype(F32) + yr[2].astype(F32)
+            G[y, z, :, LA] = G[y, z, :, LA] + total
 
     def small_z(k):
         zs, zr = S.zs, S.zr
@@ -656,112 +696,172 @@
     judge_piece(10)
     judge_piece(11)
     judge_piece(12)
+    judge_piece(13)
+    judge_piece(14)
     assemble(0)
     ag_go(0, AY, 1)
     ag_go(0, BZ, 1)
+    ag_go(0, FZ, 1, 0)
     ag_go(0, FY, 1, 0)
-    judge_piece(13)
-    arrived(XG.at[q_near], S.tk_s.at[1], S.tk_r.at[1])
+    judge_piece(15)
+    arrived(XG.at[q_near], S.tk_s.at[0], S.tk_r.at[1])
     gen_hat(q_near, 0)
     gen_hat(q_near, 1)
     gen_hat(q_near, 2)
     gen_hat(q_near, 3)
-    judge_piece(14)
-    judge_piece(15)
     judge_piece(16)
     judge_piece(17)
     assemble(1)
     ag_go(1, AY, 1)
     ag_go(1, BZ, 1)
+    ag_go(1, FZ, 1, 0)
+    ag_go(1, FY, 1, 0)
     ag_got(0, AY, 1)
     ag_go(0, AY, 2)
+    ag_go(0, FZ, 1, 1)
+    ag_go(0, FZ, 1, 2)
     ag_got(0, BZ, 1)
     ag_go(0, BZ, 2)
     ag_go(0, FY, 1, 1)
     ag_go(0, FY, 1, 7)
-    tok_far()
     ag_got(0, FY, 1, 0)
     ag_go(0, FY, 2, 0)
+    ag_got(0, FZ, 1, 0)
+    ag_go(0, FZ, 2, 0)
+    tok_far()
     assemble(2)
-    ag_go(2, BZ, 1)
     factors()
+    ag_go(2, AY, 1)
+    ag_got(1, BZ, 1)
+    ag_go(1, BZ, 2)
     ag_got(0, AY, 2)
-    ag_go(0, AZ, 1, 0)
+    ag_go(0, FZ, 1, 3)
+    ag_got(1, AY, 1)
+    ag_go(1, AY, 2)
+    ag_got(0, FZ, 1, 1)
+    ag_go(0, FZ, 2, 1)
     ag_got(0, FY, 1, 1)
     ag_go(0, FY, 2, 1)
+    ag_go(1, FY, 1, 1)
+    ag_got(0, FZ, 1, 2)
+    ag_go(0, FZ, 2, 2)
+    ag_got(0, FY, 1, 7)
+    ag_go(0, FY, 2, 7)
     ag_got(0, BZ, 2)
     ag_go(0, BZ, 3)
     ag_go(0, FY, 1, 2)
     ag_go(0, FY, 1, 6)
-    ag_go(0, AZ, 1, 1)
-    ag_got(0, FY, 1, 7)
-    ag_go(0, FY, 2, 7)
-    ag_got(0, AZ, 1, 0)
-    ag_go(0, AZ, 2, 0)
+    ag_got(0, FZ, 2, 0)
+    ag_go(0, FZ, 3, 0)
+    ag_got(0, FZ, 1, 3)
+    ag_go(0, FZ, 2, 3)
+    ag_got(2, AY, 1)
+    ag_go(2, AY, 2)
+    ag_got(1, BZ, 2)
+    ag_go(1, FY, 1, 8)
+    ag_go(1, BZ, 3)
+    ag_got(0, FZ, 2, 1)
+    ag_go(0, FZ, 3, 1)
+    ag_got(0, FZ, 2, 2)
+    ag_go(0, FZ, 3, 2)
     ag_got(0, FY, 1, 2)
     ag_go(0, FY, 2, 2)
-    ag_got(1, AY, 1)
-    ag_go(1, AY, 2)
+    ag_go(1, FY, 1, 7)
     ag_got(0, BZ, 3)
     ag_go(0, BZ, 4)
     ag_go(0, FY, 1, 3)
     ag_go(0, FY, 1, 5)
-    ag_got(1, BZ, 1)
-    ag_go(1, BZ, 2)
+    ag_got(0, FZ, 3, 0)
+    ag_go(0, FZ, 4, 0)
     ag_got(0, FY, 1, 6)
     ag_go(0, FY, 2, 6)
-    ag_got(0, AZ, 1, 1)
-    ag_go(0, AZ, 2, 1)
-    ag_go(2, AY, 1)
-    ag_got(0, FY, 1, 3)
-    ag_go(0, FY, 2, 3)
-    ag_got(0, AZ, 2, 0)
-    ag_go(0, AZ, 3, 0)
-    ag_got(0, BZ, 4)
-    ag_go(0, FY, 1, 4)
-    ag_got(0, FY, 1, 5)
-    ag_go(0, FY, 2, 5)
-    ag_got(1, BZ, 2)
-    ag_go(1, BZ, 3)
-    ag_got(2, AY, 1)
-    ag_go(2, AY, 2)
-    ag_got(0, AZ, 2, 1)
-    ag_go(0, AZ, 3, 1)
-    ag_got(0, FY, 1, 4)
-    ag_go(0, FY, 2, 4)
-    ag_got(0, AZ, 3, 0)
-    ag_go(0, AZ, 4, 0)
+    ag_got(0, FZ, 2, 3)
+    ag_go(0, FZ, 3, 3)
+    ag_got(1, FY, 1, 8)
+    ag_go(1, XY, 1, 8)
+    ag_got(1, AY, 2)
+    ag_go(1, FZ, 1, 2)
+    ag_got(0, FZ, 3, 1)
+    ag_go(0, FZ, 4, 1)
     tok_forward()
     noise_send(0)
     noise_send(1)
     noise_send(2)
+    ag_got(1, BZ, 3)
+    ag_go(1, BZ, 4)
+    ag_go(1, FY, 1, 9)
+    ag_got(0, FZ, 3, 2)
+    ag_go(0, FZ, 4, 2)
     gen_hat(q_far, 0)
     gen_hat(q_far, 1)
+    ag_go(1, FY, 2, 8)
+    ag_got(1, FZ, 1, 0)
+    ag_go(1, FZ, 2, 0)
     gen_hat(q_far, 2)
+    ag_got(0, BZ, 4)
+    ag_go(0, FY, 1, 4)
     gen_hat(q_far, 3)
-    ag_got(1, BZ, 3)
-    ag_go(1, BZ, 4)
-    ag_got(0, AZ, 3, 1)
-    ag_go(0, AZ, 4, 1)
-    ag_got(1, AY, 2)
-    ag_go(1, AZ, 1, 0)
-    arrived(XG.at[q_last], S.tk_s.at[2], S.tk_r.at[2])
+    ag_got(0, FY, 1, 3)
+    ag_go(0, FY, 2, 3)
+    ag_got(0, FZ, 3, 3)
+    ag_go(0, FZ, 4, 3)
+    ag_go(1, FZ, 1, 1)
+    ag_got(0, FY, 1, 5)
+    ag_go(0, FY, 2, 5)
+    ag_got(1, FZ, 1, 2)
+    ag_go(1, FZ, 2, 2)
+    ag_go(1, XZ, 1)
+    ag_got(1, BZ, 4)
+    ag_go(1, FY, 1, 4)
+    ag_go(2, BZ, 1)
+    arrived(XG.at[q_last], S.tk_s.at[0], S.tk_r.at[2])
     gen_hat(q_last, 0)
+    ag_got(1, FY, 1, 9)
+    ag_go(1, XY, 1, 9)
     gen_hat(q_last, 1)
-    ag_got(1, BZ, 4)
-    ag_go(1, BY, 1, 0)
-    ag_go(1, AZ, 1, 1)
+    ag_got(2, AY, 2)
+    ag_go(2, FZ, 1, 2)
     gen_hat(q_last, 2)
+    ag_go(1, FY, 2, 9)
+    ag_got(1, FY, 2, 8)
+    ag_go(1, XY, 2, 8)
     gen_hat(q_last, 3)
-    ag_got(0, AZ, 4, 0)
-    ag_got(0, AZ, 4, 1)
+    ag_got(0, FZ, 4, 0)
     product(S.H, 0, y, True)
+    ag_got(1, FZ, 2, 0)
+    ag_go(1, FZ, 3, 0)
+    ag_got(1, FY, 1, 0)
+    ag_go(1, FY, 2, 0)
+    ag_got(0, FY, 1, 4)
+    ag_go(0, FY, 2, 4)
+    ag_got(0, FZ, 4, 1)
+    product(S.H, 0, yy(1))
+    ag_got(1, FZ, 1, 1)
+    ag_go(1, FZ, 2, 1)
+    ag_got(1, FY, 1, 1)
+    ag_go(1, FY, 2, 1)
+    ag_got(0, FZ, 4, 2)
+    product(S.H, 0, yy(-1))
+    ag_got(1, FZ, 2, 2)
+    ag_go(1, FZ, 3, 2)
+    ag_go(1, XZ, 2)
+    ag_got(1, FY, 1, 7)
+    ag_go(1, FY, 2, 7)
+    ag_go(2, FZ, 1, 0)
+    ag_go(2, FY, 1, 0)
     ag_got(2, BZ, 1)
     ag_go(2, BZ, 2)
-    product(S.H, 0, yy(1))
-    product(S.H, 0, yy(-1))
-    ag_got(1, AZ, 1, 0)
-    ag_go(1, AZ, 2, 0)
+    ag_got(2, FZ, 1, 2)
+    ag_go(2, XZ, 1)
+    ag_got(1, FY, 2, 9)
+    ag_go(1, XY, 2, 9)
+    ag_got(1, FY, 1, 4)
+    ag_go(1, FY, 2, 4)
+    ag_got(1, FZ, 3, 0)
+    ag_go(1, FZ, 4, 0)
+    ag_go(2, FY, 1, 1)
+    ag_go(2, FZ, 2, 2)
+    ag_got(0, FZ, 4, 3)
     ag_got(0, FY, 2, 0)
     ag_got(0, FY, 2, 1)
     ag_got(0, FY, 2, 7)
@@ -771,161 +871,195 @@
     ag_got(0, FY, 2, 5)
     ag_got(0, FY, 2, 4)
     product(S.H, 0, yy(2))
-    ag_go(1, BY, 1, 1)
+    ag_got(1, FZ, 2, 1)
+    ag_go(1, FZ, 3, 1)
+    ag_go(2, FY, 1, 7)
     noise_wait()
     clean_rows(0)
     noisy_send(0)
     clean_rows(1)
     noisy_send(1)
+    ag_got(1, FZ, 3, 2)
+    ag_go(1, XZ, 3)
     clean_rows(2)
     noisy_send(2)
-    ag_got(1, AZ, 1, 1)
-    ag_go(1, AZ, 2, 1)
     clean_rows(3)
     noisy_send(3)
+    ag_go(1, FZ, 4, 2)
+    ag_got(2, FZ, 1, 0)
+    ag_go(2, FZ, 2, 0)
+    ag_got(2, FY, 1, 0)
+    ag_go(2, FY, 2, 0)
+    ag_go(2, FZ, 1, 1)
     ag_got(2, BZ, 2)
+    ag_go(2, FY, 1, 8)
     ag_go(2, BZ, 3)
-    ag_got(1, AZ, 2, 0)
-    ag_go(1, AZ, 3, 0)
+    ag_got(2, FY, 1, 1)
+    ag_go(2, FY, 2, 1)
+    ag_got(2, FZ, 2, 2)
+    ag_go(2, XZ, 2)
+    ag_got(1, FZ, 3, 1)
+    ag_go(1, FZ, 4, 1)
+    ag_go(2, FZ, 3, 2)
+    ag_got(2, FY, 1, 7)
+    ag_go(2, FY, 2, 7)
+    ag_got(1, FZ, 4, 2)
+    ag_go(1, XZ, 4)
     noisy_forward(0)
-    ag_got(1, BY, 1, 0)
-    ag_go(1, BY, 2, 0)
-    ag_got(1, AZ, 2, 1)
-    ag_go(1, AZ, 3, 1)
+    ag_got(2, FZ, 2, 0)
+    ag_go(2, FZ, 3, 0)
+    ag_got(2, FZ, 1, 1)
+    ag_go(2, FZ, 2, 1)
+    ag_got(2, FY, 1, 8)
+    ag_go(2, FY, 2, 8)
+    ag_go(2, XY, 1, 8)
+    noisy_wait(0)
+    judge_hats(0)
     ag_got(2, BZ, 3)
     ag_go(2, BZ, 4)
-    noisy_wait(0)
-    judge_hats(0)
-    ag_got(1, BY, 1, 1)
-    ag_go(1, BY, 2, 1)
-    ag_got(2, AY, 2)
-    ag_go(2, AZ, 1, 0)
+    ag_go(2, FY, 1, 9)
     judge_hats(1)
     noisy_forward(1)
-    ag_got(1, AZ, 3, 0)
-    ag_go(1, AZ, 4, 0)
-    ag_got(1, AZ, 3, 1)
-    ag_go(1, AZ, 4, 1)
-    ag_got(2, BZ, 4)
-    ag_go(2, BY, 1, 0)
+    ag_got(2, FZ, 3, 2)
+    ag_go(2, FZ, 4, 2)
+    ag_go(2, XZ, 3)
+    ag_got(2, FY, 2, 8)
+    ag_go(2, XY, 2, 8)
+    ag_got(2, FZ, 3, 0)
+    ag_go(2, FZ, 4, 0)
+    ag_got(2, FZ, 2, 1)
+    ag_go(2, FZ, 3, 1)
     noisy_wait(1)
     judge_hats(2)
-    ag_go(2, AZ, 1, 1)
+    ag_got(2, FY, 1, 9)
+    ag_go(2, FY, 2, 9)
+    ag_got(2, FZ, 4, 2)
+    ag_go(2, XZ, 4)
+    ag_go(2, XY, 1, 9)
+    ag_got(2, BZ, 4)
+    ag_go(2, FY, 1, 4)
     judge_hats(3)
     noisy_forward(2)
-    ag_got(2, AZ, 1, 0)
-    ag_go(2, AZ, 2, 0)
+    ag_got(1, FZ, 4, 0)
+    ag_got(1, FZ, 4, 1)
+    ag_got(1, XY, 1, 8)
+    ag_got(1, XY, 1, 9)
+    ag_got(1, XZ, 1)
+    ag_got(1, XZ, 2)
+    ag_got(1, XZ, 3)
+    ag_got(1, XZ, 4)
+    ag_got(1, XY, 2, 8)
+    ag_got(1, XY, 2, 9)
+    ag_got(1, FY, 2, 0)
+    ag_got(1, FY, 2, 1)
+    ag_got(1, FY, 2, 7)
+    ag_got(1, FY, 2, 4)
+    judged(1, 0)
+    ag_got(2, FZ, 3, 1)
+    ag_go(2, FZ, 4, 1)
+    real_rows(0)
+    ag_got(2, FY, 2, 9)
+    ag_go(2, XY, 2, 9)
     noisy_wait(2)
     judge_hats(4)
+    noisy_forward(3)
+    ag_got(2, FY, 1, 4)
+    ag_go(2, FY, 2, 4)
     judge_hats(5)
-    noisy_forward(3)
-    ag_go(2, BY, 1, 1)
-    ag_got(2, AZ, 1, 1)
-    ag_go(2, AZ, 2, 1)
-    ag_got(2, AZ, 2, 0)
-    ag_go(2, AZ, 3, 0)
     noisy_wait(3)
     judge_hats(6)
     judge_hats(7)
-    ag_got(1, AZ, 4, 0)
-    ag_got(1, AZ, 4, 1)
-    product(S.JH.at[0], 1, y, True)
-    ag_got(2, AZ, 2, 1)
-    ag_go(2, AZ, 3, 1)
-    product(S.JH.at[0], 1, yy(1))
-    product(S.JH.at[0], 1, yy(-1))
-    ag_got(2, BY, 1, 0)
-    ag_go(2, BY, 2, 0)
-    ag_got(2, AZ, 3, 0)
-    ag_go(2, AZ, 4, 0)
-    ag_got(1, BY, 2, 0)
-    ag_got(1, BY, 2, 1)
-    product(S.JH.at[0], 1, yy(2))
-    real_rows()
-    spread_rows()
+    judged(1, 1)
+    real_rows(1)
     spread_group_start()
-    ag_got(2, AZ, 3, 1)
-    ag_go(2, AZ, 4, 1)
-    ag_got(2, BY, 1, 1)
-    ag_go(2, BY, 2, 1)
+    ag_got(2, FZ, 4, 0)
+    ag_got(2, FZ, 4, 1)
+    ag_got(2, XY, 1, 8)
+    ag_got(2, XY, 1, 9)
+    ag_got(2, XZ, 1)
+    ag_got(2, XZ, 2)
+    ag_got(2, XZ, 3)
+    ag_got(2, XZ, 4)
+    ag_got(2, XY, 2, 8)
+    ag_got(2, XY, 2, 9)
+    ag_got(2, FY, 2, 0)
+    ag_got(2, FY, 2, 1)
+    ag_got(2, FY, 2, 7)
+    ag_got(2, FY, 2, 4)
+    judged(2, 0)
+    gap_rows(0)
+    judged(2, 1)
     sample_own = return_rows(S.SB, out_s, S.sm_s, S.sm_r)
-    ag_got(2, AZ, 4, 0)
-    ag_got(2, AZ, 4, 1)
-    product(S.JH.at[1], 2, y, True)
-    product(S.JH.at[1], 2, yy(1))
-    product(S.JH.at[1], 2, yy(-1))
-    ag_got(2, BY, 2, 0)
-    ag_got(2, BY, 2, 1)
-    product(S.JH.at[1], 2, yy(2))
-    gap_rows()
-    spread_z_start()
+    gap_rows(1)
     grad_b(yy(2))
     big_y0(4)
     big_y0(3)
+    big_y0(5)
+    big_y0(2)
     grad_a(yy(2))
-    big_y0(5)
     big_z(1, 0)
+    grad_b(yy(1))
+    grad_b(yy(-1))
+    spread_z_start()
     grad_a(yy(1))
-    big_y0(2)
     big_z(1, 1)
     grad_a(yy(-1))
+    big_z(1, 2)
+    big_y1(4)
+    big_z(2, 0)
+    big_y1(3)
     big_y0(6)
-    big_z(1, 2)
-    grad_a(yy(0))
     big_y0(1)
+    grad_a(y)
     big_z(1, 3)
-    grad_b(yy(1))
-    big_z(2, 0)
-    grad_b(yy(-1))
+    big_z(2, 1)
+    big_y1(5)
+    big_z(2, 2)
+    big_y1(2)
     big_y0(7)
-    big_z(2, 1)
+    big_y0(0)
     grad_b(y)
-    big_y0(0)
-    big_z(2, 2)
     spread_y_start()
-    big_y1(4)
     big_z(2, 3)
+    big_z(3, 0)
+    big_y2(4)
+    small_z(1)
+    big_y1(6)
+    big_z(3, 1)
+    spread_value()
+    dmd_rows()
+    dmd_own = return_rows(S.DB, out_d, S.dm_s, S.dm_r)
+    big_y2(3)
+    big_y2(5)
+    big_z(3, 2)
+    small_z(2)
+    big_z(3, 3)
+    big_y1(1)
+    big_z(4, 0)
+    big_y1(7)
+    big_z(4, 1)
+    big_y1(0)
+    big_y2(2)
+    big_y2(6)
+    big_z(4, 2)
+    small_z(3)
+    big_z(4, 3)
+    big_z(5, 0)
+    small_y(0)
+    big_y2(1)
+    big_y2(7)
+    small_z(4)
+    big_z(5, 1)
+    small_y(1)
+    big_z(5, 2)
+    small_y(2)
     ag_sent(0)
     ag_sent(1)
     ag_sent(2)
-    big_z(3, 0)
-    big_y1(3)
-    big_z(3, 1)
-    spread_value()
-    dmd_rows()
-    big_y1(5)
-    big_z(3, 2)
-    dmd_own = return_rows(S.DB, out_d, S.dm_s, S.dm_r)
-    big_z(3, 3)
-    big_y2(4)
-    small_z(1)
-    big_y1(2)
-    big_z(4, 0)
-    big_y2(3)
-    big_y1(6)
-    big_z(4, 1)
-    big_y2(5)
-    big_y1(1)
-    big_z(4, 2)
-    small_z(2)
-    big_y2(2)
-    big_y1(7)
-    big_z(5, 0)
-    small_y(0)
-    drain()
-    big_z(4, 3)
-    big_y2(6)
-    big_z(5, 1)
-    big_y1(0)
-    big_z(5, 2)
-    big_y2(1)
-    small_z(3)
-    big_y2(7)
-    small_y(1)
+    sample_own.wait()
     big_z(5, 3)
     big_y2(0)
-    small_z(4)
-    small_y(2)
+    small_y(3)
     small_z(5)
     GF, OW = S.GF, S.OW
     done = G[y, z] / S.SV[0:1, 0:1] / TOKENS
@@ -934,12 +1068,13 @@
         return remote(GF.at[row], OW.at[slot], S.ow_s.at[row], S.ow_r.at[slot], target)
 
     for row in range(2):
-        GF[row] = done[row * HALF : (row + 1) * HALF]
+        part = jnp.concatenate([done[row * HALF : (row + 1) * HALF], jnp.zeros((PAD - HALF, COLS), F32)], axis=0)
+        GF[row] = part.astype(BF16)
 
     @pl.when(l == 0)
     def _():
+        own_row(1, 0, dev(h, c, y, z, 1)).start()
         OW[0] = GF[0]
-        own_row(1, 0, dev(h, c, y, z, 1)).start()
 
     @pl.when(l == 1)
     def _():
@@ -948,10 +1083,9 @@
         arrived(OW.at[0], S.ow_s.at[0], S.ow_r.at[0])
 
     arrived(OW.at[1], S.ow_s.at[1], S.ow_r.at[1])
-    out_w[...] = OW[0] + OW[1]
+    out_w[...] = (OW[0].astype(F32) + OW[1].astype(F32))[:HALF]
     return_wait(out_s, S.sm_s, S.sm_r)
     return_wait(out_d, S.dm_s, S.dm_r)
-    sample_own.wait()
     dmd_own.wait()
     rings_sent()
     drain()

time: 122 us -> 113 us (0.926)
  Pallas kernels: 119 us -> 111 us
    pallas_call x1, Pallas kernels: 117 us -> 109 us  [on_device(): pl.pallas_call(kernel, out_shape=out_shape, in_specs=[hbm, hbm, smem, vme...]
where the time goes in v3:
time: 113 us; the launch traced here: 112 us
  Pallas kernels  111 us (98%)
    pallas_call x1, Pallas kernels, on_device(): pl.pallas_call(kernel, out_shape=out_shape, in_specs=[hbm, hbm, smem, vme...  109 us

profile of v3, /device:TPU:8, one launch (start us, length us, event | category | flops | bytes accessed | tf_op | source)
XLA Modules:
  0.0 112.1 jit_solution(17388250843778277066)
XLA Ops:
  0.6 109.1 %shard_map.121 = (bf16[128,2560]{1,0:T(8,128)(2,1)}, bf16[128,2560]{1,0:T(8,128)(2,1)}, f32[40,640]{1,0:T(8,128)}) custom-call(bf16[128,2560]{1,0:T(8,128)(2,1)} %gi.1, bf16[128,2560]{1,0:T(8,128)(2,1)} %noise.1, s32[2]{0:T(128)} %dstep.1, s32[2,3]{1,0:T(2,128)} %bitcast.1, bf16[40,640]{1,0:T(8,128)(2,1)} %wg.1, bf16[40,640]{1,0:T(8,128)(2,1)} %wt.1, ...), custom_call_target="tpu_custom_call" | custom-call | tf_op jit(solution)/shard_map/pallas_call | solution.py:1123
  109.7 2.2 %shard_map.122 = (bf16[128,2560]{1,0:T(8,128)(2,1)}, bf16[128,2560]{1,0:T(8,128)(2,1)}, f32[40,640]{1,0:T(8,128)}) custom-call(bf16[128,2560]{1,0:T(8,128)(2,1)} %get-tuple-element.6.a_in, bf16[128,2560]{1,0:T(8,128)(2,1)} %get-tuple-element.7.b_in, f32[40,640]{1,0:T(8,128)} %get-tuple-element.8.c_in), custom_call_target="tpu_custom_call" | custom-call | tf_op jit(solution)/shard_map/pallas_call | solution.py:1135

commit v4 on v3

--- a/solution.py
+++ b/solution.py
@@ -714,7 +714,6 @@
     assemble(1)
     ag_go(1, AY, 1)
     ag_go(1, BZ, 1)
-    ag_go(1, FZ, 1, 0)
     ag_go(1, FY, 1, 0)
     ag_got(0, AY, 1)
     ag_go(0, AY, 2)
@@ -724,143 +723,130 @@
     ag_go(0, BZ, 2)
     ag_go(0, FY, 1, 1)
     ag_go(0, FY, 1, 7)
+    tok_far()
+    assemble(2)
+    ag_got(0, FZ, 1, 0)
+    ag_go(0, FZ, 2, 0)
+    factors()
     ag_got(0, FY, 1, 0)
     ag_go(0, FY, 2, 0)
-    ag_got(0, FZ, 1, 0)
-    ag_go(0, FZ, 2, 0)
-    tok_far()
-    assemble(2)
-    factors()
-    ag_go(2, AY, 1)
     ag_got(1, BZ, 1)
     ag_go(1, BZ, 2)
-    ag_got(0, AY, 2)
-    ag_go(0, FZ, 1, 3)
+    ag_go(2, AY, 1)
+    ag_got(0, FZ, 1, 1)
+    ag_go(0, FZ, 2, 1)
     ag_got(1, AY, 1)
     ag_go(1, AY, 2)
-    ag_got(0, FZ, 1, 1)
-    ag_go(0, FZ, 2, 1)
+    ag_got(0, FZ, 1, 2)
+    ag_go(0, FZ, 2, 2)
     ag_got(0, FY, 1, 1)
     ag_go(0, FY, 2, 1)
-    ag_go(1, FY, 1, 1)
-    ag_got(0, FZ, 1, 2)
-    ag_go(0, FZ, 2, 2)
-    ag_got(0, FY, 1, 7)
-    ag_go(0, FY, 2, 7)
     ag_got(0, BZ, 2)
     ag_go(0, BZ, 3)
     ag_go(0, FY, 1, 2)
     ag_go(0, FY, 1, 6)
     ag_got(0, FZ, 2, 0)
     ag_go(0, FZ, 3, 0)
-    ag_got(0, FZ, 1, 3)
-    ag_go(0, FZ, 2, 3)
+    ag_got(0, AY, 2)
+    ag_go(0, FZ, 1, 3)
+    ag_got(0, FY, 1, 7)
+    ag_go(0, FY, 2, 7)
+    ag_got(0, FZ, 2, 1)
+    ag_go(0, FZ, 3, 1)
     ag_got(2, AY, 1)
     ag_go(2, AY, 2)
-    ag_got(1, BZ, 2)
-    ag_go(1, FY, 1, 8)
-    ag_go(1, BZ, 3)
-    ag_got(0, FZ, 2, 1)
-    ag_go(0, FZ, 3, 1)
     ag_got(0, FZ, 2, 2)
     ag_go(0, FZ, 3, 2)
     ag_got(0, FY, 1, 2)
     ag_go(0, FY, 2, 2)
-    ag_go(1, FY, 1, 7)
+    ag_got(1, BZ, 2)
+    ag_go(1, FY, 1, 8)
     ag_got(0, BZ, 3)
     ag_go(0, BZ, 4)
     ag_go(0, FY, 1, 3)
-    ag_go(0, FY, 1, 5)
     ag_got(0, FZ, 3, 0)
     ag_go(0, FZ, 4, 0)
+    ag_go(0, FY, 1, 5)
+    ag_go(1, BZ, 3)
+    ag_got(0, FZ, 1, 3)
+    ag_go(0, FZ, 2, 3)
     ag_got(0, FY, 1, 6)
     ag_go(0, FY, 2, 6)
-    ag_got(0, FZ, 2, 3)
-    ag_go(0, FZ, 3, 3)
+    ag_got(0, FZ, 3, 1)
+    ag_go(0, FZ, 4, 1)
+    ag_got(0, FZ, 3, 2)
+    ag_go(0, FZ, 4, 2)
     ag_got(1, FY, 1, 8)
     ag_go(1, XY, 1, 8)
+    ag_got(0, BZ, 4)
+    ag_go(0, FY, 1, 4)
     ag_got(1, AY, 2)
     ag_go(1, FZ, 1, 2)
-    ag_got(0, FZ, 3, 1)
-    ag_go(0, FZ, 4, 1)
+    ag_got(0, FY, 1, 3)
+    ag_go(0, FY, 2, 3)
+    ag_got(1, BZ, 3)
+    ag_go(1, BZ, 4)
     tok_forward()
     noise_send(0)
     noise_send(1)
     noise_send(2)
-    ag_got(1, BZ, 3)
-    ag_go(1, BZ, 4)
+    ag_got(0, FY, 1, 5)
+    ag_go(0, FY, 2, 5)
+    ag_go(1, FZ, 1, 0)
+    gen_hat(q_far, 0)
+    ag_got(0, FZ, 2, 3)
+    ag_go(0, FZ, 3, 3)
     ag_go(1, FY, 1, 9)
-    ag_got(0, FZ, 3, 2)
-    ag_go(0, FZ, 4, 2)
-    gen_hat(q_far, 0)
     gen_hat(q_far, 1)
+    gen_hat(q_far, 2)
+    gen_hat(q_far, 3)
     ag_go(1, FY, 2, 8)
+    ag_go(1, FZ, 1, 1)
+    ag_got(0, FY, 1, 4)
+    ag_go(0, FY, 2, 4)
+    ag_got(1, FZ, 1, 2)
+    ag_go(1, XZ, 1)
+    ag_go(1, FZ, 2, 2)
+    ag_go(1, FY, 1, 1)
+    ag_go(2, BZ, 1)
+    ag_go(1, FY, 1, 7)
     ag_got(1, FZ, 1, 0)
     ag_go(1, FZ, 2, 0)
-    gen_hat(q_far, 2)
-    ag_got(0, BZ, 4)
-    ag_go(0, FY, 1, 4)
-    gen_hat(q_far, 3)
-    ag_got(0, FY, 1, 3)
-    ag_go(0, FY, 2, 3)
     ag_got(0, FZ, 3, 3)
     ag_go(0, FZ, 4, 3)
-    ag_go(1, FZ, 1, 1)
-    ag_got(0, FY, 1, 5)
-    ag_go(0, FY, 2, 5)
-    ag_got(1, FZ, 1, 2)
-    ag_go(1, FZ, 2, 2)
-    ag_go(1, XZ, 1)
-    ag_got(1, BZ, 4)
-    ag_go(1, FY, 1, 4)
-    ag_go(2, BZ, 1)
     arrived(XG.at[q_last], S.tk_s.at[0], S.tk_r.at[2])
     gen_hat(q_last, 0)
     ag_got(1, FY, 1, 9)
     ag_go(1, XY, 1, 9)
     gen_hat(q_last, 1)
-    ag_got(2, AY, 2)
-    ag_go(2, FZ, 1, 2)
     gen_hat(q_last, 2)
+    gen_hat(q_last, 3)
     ag_go(1, FY, 2, 9)
-    ag_got(1, FY, 2, 8)
-    ag_go(1, XY, 2, 8)
-    gen_hat(q_last, 3)
     ag_got(0, FZ, 4, 0)
     product(S.H, 0, y, True)
-    ag_got(1, FZ, 2, 0)
-    ag_go(1, FZ, 3, 0)
-    ag_got(1, FY, 1, 0)
-    ag_go(1, FY, 2, 0)
-    ag_got(0, FY, 1, 4)
-    ag_go(0, FY, 2, 4)
+    ag_got(1, FZ, 2, 2)
+    ag_go(1, FZ, 3, 2)
+    ag_go(1, XZ, 2)
+    ag_got(1, BZ, 4)
+    ag_go(1, FY, 1, 4)
     ag_got(0, FZ, 4, 1)
     product(S.H, 0, yy(1))
     ag_got(1, FZ, 1, 1)
     ag_go(1, FZ, 2, 1)
+    ag_got(0, FZ, 4, 2)
+    product(S.H, 0, yy(-1))
+    ag_got(1, FY, 2, 8)
+    ag_go(1, XY, 2, 8)
+    ag_got(1, FY, 1, 0)
+    ag_go(1, FY, 2, 0)
     ag_got(1, FY, 1, 1)
     ag_go(1, FY, 2, 1)
-    ag_got(0, FZ, 4, 2)
-    product(S.H, 0, yy(-1))
-    ag_got(1, FZ, 2, 2)
-    ag_go(1, FZ, 3, 2)
-    ag_go(1, XZ, 2)
+    ag_got(2, BZ, 1)
+    ag_go(2, BZ, 2)
+    ag_got(1, FZ, 2, 0)
+    ag_go(1, FZ, 3, 0)
     ag_got(1, FY, 1, 7)
     ag_go(1, FY, 2, 7)
-    ag_go(2, FZ, 1, 0)
-    ag_go(2, FY, 1, 0)
-    ag_got(2, BZ, 1)
-    ag_go(2, BZ, 2)
-    ag_got(2, FZ, 1, 2)
-    ag_go(2, XZ, 1)
-    ag_got(1, FY, 2, 9)
-    ag_go(1, XY, 2, 9)
-    ag_got(1, FY, 1, 4)
-    ag_go(1, FY, 2, 4)
-    ag_got(1, FZ, 3, 0)
-    ag_go(1, FZ, 4, 0)
-    ag_go(2, FY, 1, 1)
-    ag_go(2, FZ, 2, 2)
     ag_got(0, FZ, 4, 3)
     ag_got(0, FY, 2, 0)
     ag_got(0, FY, 2, 1)
@@ -871,75 +857,82 @@
     ag_got(0, FY, 2, 5)
     ag_got(0, FY, 2, 4)
     product(S.H, 0, yy(2))
-    ag_got(1, FZ, 2, 1)
-    ag_go(1, FZ, 3, 1)
-    ag_go(2, FY, 1, 7)
+    ag_got(1, FZ, 3, 2)
+    ag_go(1, FZ, 4, 2)
+    ag_go(1, XZ, 3)
+    ag_go(2, FY, 1, 0)
     noise_wait()
     clean_rows(0)
     noisy_send(0)
     clean_rows(1)
     noisy_send(1)
-    ag_got(1, FZ, 3, 2)
-    ag_go(1, XZ, 3)
     clean_rows(2)
     noisy_send(2)
+    ag_got(2, AY, 2)
+    ag_go(2, FZ, 1, 2)
     clean_rows(3)
     noisy_send(3)
-    ag_go(1, FZ, 4, 2)
+    ag_got(1, FY, 2, 9)
+    ag_go(1, XY, 2, 9)
+    ag_got(1, FY, 1, 4)
+    ag_go(1, FY, 2, 4)
+    ag_got(1, FZ, 2, 1)
+    ag_go(1, FZ, 3, 1)
+    ag_go(2, FZ, 1, 0)
+    ag_got(2, BZ, 2)
+    ag_go(2, FY, 1, 8)
+    ag_got(1, FZ, 3, 0)
+    ag_go(1, FZ, 4, 0)
+    ag_go(2, FY, 1, 1)
+    ag_got(1, FZ, 4, 2)
+    ag_go(1, XZ, 4)
+    ag_go(2, BZ, 3)
+    ag_got(2, FZ, 1, 2)
+    ag_go(2, XZ, 1)
+    ag_go(2, FY, 1, 7)
+    ag_go(2, FZ, 2, 2)
+    noisy_forward(0)
+    ag_got(1, FZ, 3, 1)
+    ag_go(1, FZ, 4, 1)
+    ag_got(2, FY, 1, 8)
+    ag_go(2, FY, 2, 8)
+    ag_go(2, XY, 1, 8)
     ag_got(2, FZ, 1, 0)
     ag_go(2, FZ, 2, 0)
     ag_got(2, FY, 1, 0)
     ag_go(2, FY, 2, 0)
     ag_go(2, FZ, 1, 1)
-    ag_got(2, BZ, 2)
-    ag_go(2, FY, 1, 8)
-    ag_go(2, BZ, 3)
     ag_got(2, FY, 1, 1)
     ag_go(2, FY, 2, 1)
+    ag_got(2, BZ, 3)
+    ag_go(2, BZ, 4)
+    ag_go(2, FY, 1, 9)
+    noisy_wait(0)
+    judge_hats(0)
+    judge_hats(1)
+    noisy_forward(1)
     ag_got(2, FZ, 2, 2)
+    ag_go(2, FZ, 3, 2)
     ag_go(2, XZ, 2)
-    ag_got(1, FZ, 3, 1)
-    ag_go(1, FZ, 4, 1)
-    ag_go(2, FZ, 3, 2)
     ag_got(2, FY, 1, 7)
     ag_go(2, FY, 2, 7)
-    ag_got(1, FZ, 4, 2)
-    ag_go(1, XZ, 4)
-    noisy_forward(0)
+    ag_got(2, FY, 2, 8)
+    ag_go(2, XY, 2, 8)
     ag_got(2, FZ, 2, 0)
     ag_go(2, FZ, 3, 0)
     ag_got(2, FZ, 1, 1)
     ag_go(2, FZ, 2, 1)
-    ag_got(2, FY, 1, 8)
-    ag_go(2, FY, 2, 8)
-    ag_go(2, XY, 1, 8)
-    noisy_wait(0)
-    judge_hats(0)
-    ag_got(2, BZ, 3)
-    ag_go(2, BZ, 4)
-    ag_go(2, FY, 1, 9)
-    judge_hats(1)
-    noisy_forward(1)
-    ag_got(2, FZ, 3, 2)
-    ag_go(2, FZ, 4, 2)
-    ag_go(2, XZ, 3)
-    ag_got(2, FY, 2, 8)
-    ag_go(2, XY, 2, 8)
-    ag_got(2, FZ, 3, 0)
-    ag_go(2, FZ, 4, 0)
-    ag_got(2, FZ, 2, 1)
-    ag_go(2, FZ, 3, 1)
+    ag_got(2, BZ, 4)
+    ag_go(2, FY, 1, 4)
     noisy_wait(1)
     judge_hats(2)
     ag_got(2, FY, 1, 9)
     ag_go(2, FY, 2, 9)
-    ag_got(2, FZ, 4, 2)
-    ag_go(2, XZ, 4)
     ag_go(2, XY, 1, 9)
-    ag_got(2, BZ, 4)
-    ag_go(2, FY, 1, 4)
     judge_hats(3)
     noisy_forward(2)
+    ag_got(2, FZ, 3, 2)
+    ag_go(2, FZ, 4, 2)
     ag_got(1, FZ, 4, 0)
     ag_got(1, FZ, 4, 1)
     ag_got(1, XY, 1, 8)
@@ -955,17 +948,24 @@
     ag_got(1, FY, 2, 7)
     ag_got(1, FY, 2, 4)
     judged(1, 0)
-    ag_got(2, FZ, 3, 1)
-    ag_go(2, FZ, 4, 1)
+    ag_go(2, XZ, 3)
+    ag_got(2, FZ, 3, 0)
+    ag_go(2, FZ, 4, 0)
+    ag_got(2, FZ, 2, 1)
+    ag_go(2, FZ, 3, 1)
     real_rows(0)
-    ag_got(2, FY, 2, 9)
-    ag_go(2, XY, 2, 9)
+    ag_got(2, FY, 1, 4)
+    ag_go(2, FY, 2, 4)
+    ag_got(2, FZ, 4, 2)
+    ag_go(2, XZ, 4)
     noisy_wait(2)
     judge_hats(4)
     noisy_forward(3)
-    ag_got(2, FY, 1, 4)
-    ag_go(2, FY, 2, 4)
     judge_hats(5)
+    ag_got(2, FY, 2, 9)
+    ag_go(2, XY, 2, 9)
+    ag_got(2, FZ, 3, 1)
+    ag_go(2, FZ, 4, 1)
     noisy_wait(3)
     judge_hats(6)
     judge_hats(7)
@@ -990,6 +990,7 @@
     gap_rows(0)
     judged(2, 1)
     sample_own = return_rows(S.SB, out_s, S.sm_s, S.sm_r)
+    spread_z_start()
     gap_rows(1)
     grad_b(yy(2))
     big_y0(4)
@@ -1000,7 +1001,6 @@
     big_z(1, 0)
     grad_b(yy(1))
     grad_b(yy(-1))
-    spread_z_start()
     grad_a(yy(1))
     big_z(1, 1)
     grad_a(yy(-1))
@@ -1012,6 +1012,7 @@
     big_y0(1)
     grad_a(y)
     big_z(1, 3)
+    spread_y_start()
     big_z(2, 1)
     big_y1(5)
     big_z(2, 2)
@@ -1019,20 +1020,19 @@
     big_y0(7)
     big_y0(0)
     grad_b(y)
-    spread_y_start()
     big_z(2, 3)
     big_z(3, 0)
     big_y2(4)
     small_z(1)
     big_y1(6)
     big_z(3, 1)
+    big_y2(3)
+    big_y2(5)
+    small_z(2)
     spread_value()
     dmd_rows()
     dmd_own = return_rows(S.DB, out_d, S.dm_s, S.dm_r)
-    big_y2(3)
-    big_y2(5)
     big_z(3, 2)
-    small_z(2)
     big_z(3, 3)
     big_y1(1)
     big_z(4, 0)
@@ -1041,18 +1041,18 @@
     big_y1(0)
     big_y2(2)
     big_y2(6)
+    small_z(3)
     big_z(4, 2)
-    small_z(3)
     big_z(4, 3)
     big_z(5, 0)
     small_y(0)
     big_y2(1)
     big_y2(7)
-    small_z(4)
     big_z(5, 1)
     small_y(1)
     big_z(5, 2)
     small_y(2)
+    small_z(4)
     ag_sent(0)
     ag_sent(1)
     ag_sent(2)
@@ -1105,10 +1105,24 @@
         own_row(1, 1, dev(oh, c, y, z, 1)).wait_send()
 
 
-def copy_results(a_in, b_in, c_in, a_out, b_out, c_out):
-    a_out[...] = a_in[...]
-    b_out[...] = b_in[...]
-    c_out[...] = c_in[...]
+def copy_results(*refs):
+    ins, outs, held, come, gone = refs[:3], refs[3:6], refs[6:9], refs[9], refs[10]
+    first, second = [], []
+    for source, buffer, target in zip(ins, held, outs):
+        rows = min(source.shape[0], ROWS // 4)
+        rows = rows if source.shape[0] % rows == 0 else source.shape[0]
+        for i in range(source.shape[0] // rows):
+            at = pl.ds(i * rows, rows)
+            n = len(first)
+            first.append(pltpu.make_async_copy(source.at[at], buffer.at[at], come.at[n]))
+            second.append(pltpu.make_async_copy(buffer.at[at], target.at[at], gone.at[n]))
+    for copy in first:
+        copy.start()
+    for copy, after in zip(first, second):
+        copy.wait()
+        after.start()
+    for after in second:
+        after.wait()
 
 
 def on_device(gi, noise, dmd_step, scale_group, wg, wt, wc, scales, mod, tproj):
@@ -1130,14 +1144,12 @@
             collective_id=0, has_side_effects=True, vmem_limit_bytes=64 * 1024 * 1024 - 65536
         ),
     )(gi, noise, dmd_step, scale_group.T, wg, wt, wc, scales, mod, tproj)
-    half = pl.BlockSpec((ROWS // 2, D), lambda i: (i, 0))
-    whole = pl.BlockSpec((HALF, COLS), lambda i: (0, 0))
     return pl.pallas_call(
         copy_results,
-        grid=(2,),
         out_shape=out_shape,
-        in_specs=[half, half, whole],
-        out_specs=(half, half, whole),
+        in_specs=[hbm] * 3,
+        out_specs=(hbm,) * 3,
+        scratch_shapes=[pltpu.VMEM(s.shape, s.dtype) for s in out_shape] + [pltpu.SemaphoreType.DMA((9,))] * 2,
     )(*results)
 
 

time: 113 us -> 111 us (0.982)
    pallas_call x1, Pallas kernels: 109 us -> 107 us  [on_device(): pl.pallas_call(kernel, out_shape=out_shape, in_specs=[hbm, hbm, smem, vme...]
where the time goes in v4:
time: 111 us; the launch traced here: 110 us
  Pallas kernels  110 us (99%)
    pallas_call x1, Pallas kernels, on_device(): pl.pallas_call(kernel, out_shape=out_shape, in_specs=[hbm, hbm, smem, vme...  107 us
    pallas_call x1, Pallas kernels, on_device(): pl.pallas_call(copy_results, out_shape=out_shape, in_specs=[hbm] * 3, out...  2.25 us

profile of v4, /device:TPU:8, one launch (start us, length us, event | category | flops | bytes accessed | tf_op | source)
XLA Modules:
  0.0 110.3 jit_solution(15309203213550804126)
XLA Ops:
  0.6 107.3 %shard_map.121 = (bf16[128,2560]{1,0:T(8,128)(2,1)}, bf16[128,2560]{1,0:T(8,128)(2,1)}, f32[40,640]{1,0:T(8,128)}) custom-call(bf16[128,2560]{1,0:T(8,128)(2,1)} %gi.1, bf16[128,2560]{1,0:T(8,128)(2,1)} %noise.1, s32[2]{0:T(128)} %dstep.1, s32[2,3]{1,0:T(2,128)} %bitcast.1, bf16[40,640]{1,0:T(8,128)(2,1)} %wg.1, bf16[40,640]{1,0:T(8,128)(2,1)} %wt.1, ...), custom_call_target="tpu_custom_call" | custom-call | tf_op jit(solution)/shard_map/pallas_call | solution.py:1137
  107.9 2.3 %shard_map.122 = (bf16[128,2560]{1,0:T(8,128)(2,1)}, bf16[128,2560]{1,0:T(8,128)(2,1)}, f32[40,640]{1,0:T(8,128)}) custom-call(bf16[128,2560]{1,0:T(8,128)(2,1)} %get-tuple-element.6.refs_0_, bf16[128,2560]{1,0:T(8,128)(2,1)} %get-tuple-element.7.refs_1_, f32[40,640]{1,0:T(8,128)} %get-tuple-element.8.refs_2_), custom_call_target="tpu_custom_call" | custom-call | tf_op jit(solution)/shard_map/pallas_call | solution.py:1147

commit v5 on v4

--- a/solution.py
+++ b/solution.py
@@ -297,8 +297,8 @@
 
         @pl.when(l == 1)
         def _():
+            x_first(m, 1).start()
             x_second(m).start()
-            x_first(m, 1).start()
 
     def assemble(m):
         @pl.when(l == 1)

time: 111 us -> 110 us (level)
  no operation moved by 1% of the time
where the time goes in v5:
time: 110 us
  Pallas kernels  109 us (99%)
    pallas_call x1, Pallas kernels, on_device(): pl.pallas_call(kernel, out_shape=out_shape, in_specs=[hbm, hbm, smem, vme...  107 us
    pallas_call x1, Pallas kernels, on_device(): pl.pallas_call(copy_results, out_shape=out_shape, in_specs=[hbm] * 3, out...  2.25 us

profile of v5, /device:TPU:8, one launch (start us, length us, event | category | flops | bytes accessed | tf_op | source)
XLA Modules:
  0.0 109.8 jit_solution(3990034379300351870)
XLA Ops:
  0.6 106.8 %shard_map.121 = (bf16[128,2560]{1,0:T(8,128)(2,1)}, bf16[128,2560]{1,0:T(8,128)(2,1)}, f32[40,640]{1,0:T(8,128)}) custom-call(bf16[128,2560]{1,0:T(8,128)(2,1)} %gi.1, bf16[128,2560]{1,0:T(8,128)(2,1)} %noise.1, s32[2]{0:T(128)} %dstep.1, s32[2,3]{1,0:T(2,128)} %bitcast.1, bf16[40,640]{1,0:T(8,128)(2,1)} %wg.1, bf16[40,640]{1,0:T(8,128)(2,1)} %wt.1, ...), custom_call_target="tpu_custom_call" | custom-call | tf_op jit(solution)/shard_map/pallas_call | solution.py:1137
  107.4 2.3 %shard_map.122 = (bf16[128,2560]{1,0:T(8,128)(2,1)}, bf16[128,2560]{1,0:T(8,128)(2,1)}, f32[40,640]{1,0:T(8,128)}) custom-call(bf16[128,2560]{1,0:T(8,128)(2,1)} %get-tuple-element.6.refs_0_, bf16[128,2560]{1,0:T(8,128)(2,1)} %get-tuple-element.7.refs_1_, f32[40,640]{1,0:T(8,128)} %get-tuple-element.8.refs_2_), custom_call_target="tpu_custom_call" | custom-call | tf_op jit(solution)/shard_map/pallas_call | solution.py:1147

commit v6 on v5

--- a/solution.py
+++ b/solution.py
@@ -46,7 +46,11 @@
             continue
         steps += [(m, FZ, k, i) for k in (1, 2, 3, 4) for i in range(4)] if m in FINE_Z else [(m, AZ, k, i) for k in (1, 2, 3, 4) for i in range(2)]
         steps += [(m, FY, k, i) for k in (1, 2) for i in range(8)] if m in FINE_Y else [(m, BY, k, i) for k in (1, 2) for i in range(2)]
-    return {step: n for n, step in enumerate(steps)}
+    numbers, table = {}, {}
+    for m, op, k, i in steps:
+        key = (m, op) if op in (XY, XZ) else (m, op, k) if op == FY and k == 2 and i < 8 else (m, op, k, i)
+        table[m, op, k, i] = numbers.setdefault(key, len(numbers))
+    return table
 
 
 AG_SEMS = ag_table()
@@ -95,7 +99,7 @@
         GF=vmem((2, PAD, COLS), BF16),
         OW=vmem((2, PAD, COLS), BF16),
         ag_s=dma((3, 6)),
-        ag_r=dma((len(AG_SEMS),)),
+        ag_r=dma((len(set(AG_SEMS.values())),)),
         x_s=dma((3, 2)),
         x_r=dma((3, 2)),
         tk_s=dma((2,)),
@@ -249,6 +253,14 @@
     def ag_got(m, op, k, i=0):
         W = S.W
         ss, rs = ag_sems(m, op, k, i)
+        if op == XZ or op == XY or (op == FY and k == 2 and i < 8):
+            if op == XZ and k == 4:
+                arrived(W.at[m, 0, 0:7, :, LA], ss, rs)
+            elif op == XY and k == 2 and i == 9:
+                arrived(W.at[m, 0, 0:6, :, LB], ss, rs)
+            elif op == FY and i == 4:
+                arrived(W.at[m, 0, 0:4, :, LB] if m in SHARED else W.at[m, 0, :, :, LB], ss, rs)
+            return
         if op == AY:
             both = W.at[m, 0:2, z, :, LA] if k == 1 else W.at[m, 0, z, :, LA]
         elif op == AZ:

time: 110 us -> 110 us (level)
  no operation moved by 1% of the time
where the time goes in v6:
time: 110 us
  Pallas kernels  109 us (99%)
    pallas_call x1, Pallas kernels, on_device(): pl.pallas_call(kernel, out_shape=out_shape, in_specs=[hbm, hbm, smem, vme...  107 us
    pallas_call x1, Pallas kernels, on_device(): pl.pallas_call(copy_results, out_shape=out_shape, in_specs=[hbm] * 3, out...  2.25 us

profile of v6, /device:TPU:8, one launch (start us, length us, event | category | flops | bytes accessed | tf_op | source)
XLA Modules:
  0.0 109.6 jit_solution(2113599266754701070)
XLA Ops:
  0.6 106.6 %shard_map.121 = (bf16[128,2560]{1,0:T(8,128)(2,1)}, bf16[128,2560]{1,0:T(8,128)(2,1)}, f32[40,640]{1,0:T(8,128)}) custom-call(bf16[128,2560]{1,0:T(8,128)(2,1)} %gi.1, bf16[128,2560]{1,0:T(8,128)(2,1)} %noise.1, s32[2]{0:T(128)} %dstep.1, s32[2,3]{1,0:T(2,128)} %bitcast.1, bf16[40,640]{1,0:T(8,128)(2,1)} %wg.1, bf16[40,640]{1,0:T(8,128)(2,1)} %wt.1, ...), custom_call_target="tpu_custom_call" | custom-call | tf_op jit(solution)/shard_map/pallas_call | solution.py:1149
  107.2 2.3 %shard_map.122 = (bf16[128,2560]{1,0:T(8,128)(2,1)}, bf16[128,2560]{1,0:T(8,128)(2,1)}, f32[40,640]{1,0:T(8,128)}) custom-call(bf16[128,2560]{1,0:T(8,128)(2,1)} %get-tuple-element.6.refs_0_, bf16[128,2560]{1,0:T(8,128)(2,1)} %get-tuple-element.7.refs_1_, f32[40,640]{1,0:T(8,128)} %get-tuple-element.8.refs_2_), custom_call_target="tpu_custom_call" | custom-call | tf_op jit(solution)/shard_map/pallas_call | solution.py:1159
